TPU v7x, 512 devices: a whole 4x4x16 slice. The times are simulated.
512 devices in a mesh: wide: 128 (over x, z, core), grp: 4 (over y).
Axes of the slice: x: 4, y: 4, z: 16, core: 2. Of those that a mesh axis runs over, the one named last changes fastest.
Arguments:
- query_rows: bfloat16 [65536, 1280], P(('wide', 'grp')), may hold values from -9 to 9, as said below
- key_rows: bfloat16 [65536, 1280], P(('wide', 'grp')), may hold values from -9 to 9, as said below
- value_rows: bfloat16 [65536, 1280], P(('wide', 'grp')), may hold values from -6 to 6
- block_image: int32 [512], replicated, may hold values from 0 to 126, never falling along the last dimension, each value on 1 to 8 neighbouring positions
Outputs:
- attended: bfloat16 [65536, 1280], P(('wide', 'grp'))
Inputs may be any that keep to these rules, and one draw needn't show every extreme that they name: `query_rows`: Queries: entries bounded as stated. `key_rows`: Keys: entries bounded as stated. `block_image`: image numbers never fall along the window; every image covers 1 to 8 whole blocks and one covers exactly 8.
All inputs are finite; a program needn't handle non-finite values.
Results may differ from a plain program's by a relative error of at most 0.004.
Values may be sent and summed in bfloat16 or wider, within the bound.
No kernel may reach another device: no remote copies, remote signals or barrier semaphores. Data moves between devices by JAX's collectives and lax.ppermute only.
A program may use at most 64 MiB of HBM per device.

v0:
```python
import math

import jax
import jax.numpy as jnp
from jax import lax
from jax.sharding import PartitionSpec as P

HDIM = 80
BLK = 128
MOST = 8


neg_large = -1e30


def from_behind(value, axis, steps):
    count = lax.axis_size(axis)
    leading, last = (max(0, -steps), min(count, count - steps))
    return lax.ppermute(value, axis, [(source, source + steps) for source in range(leading, last)])


def block_tokens(block_ids, block_rows):
    return jnp.broadcast_to(block_ids[:, None], (block_ids.shape[0], block_rows)).reshape(-1)


def fold_tile(totals, query_ids, query_head, key_head, value_head, key_ids, scale_value):
    live_pairs = query_ids[:, None] == key_ids[None, :]
    acc_out, run_max, run_den = totals
    scores = (
        jnp.einsum("qhd,khd->qhk", query_head, key_head, preferred_element_type=jnp.float32)
        * scale_value
    )
    scores = jnp.where(live_pairs[:, None, :], scores, neg_large)
    new_max = jnp.maximum(run_max, jnp.max(scores, axis=-1))
    weights = jnp.where(live_pairs[:, None, :], jnp.exp(scores - new_max[..., None]), 0.0)
    fading = jnp.exp(run_max - new_max)
    run_den = run_den * fading + jnp.sum(weights, axis=-1)
    acc_out = acc_out * fading[..., None] + jnp.einsum(
        "qhk,khd->qhd", weights.astype(jnp.bfloat16), value_head, preferred_element_type=jnp.float32
    )
    return (acc_out, new_max, run_den)


def fold_keys(totals, query_ids, query_head, key_head, value_head, key_ids, scale_value):
    current = tuple((member for member in totals))
    current = fold_tile(current, query_ids, query_head, key_head, value_head, key_ids, scale_value)
    return current


def body(query_rows, key_rows, value_rows, block_image):
    stacked = jnp.stack((query_rows, key_rows, value_rows))
    regrouped = lax.all_to_all(stacked, "grp", split_axis=2, concat_axis=1, tiled=True)
    local_rows = regrouped.shape[1]
    head_count = regrouped.shape[2] // HDIM
    shaped = regrouped.reshape(3, local_rows, head_count, HDIM)
    query_head = shaped[0]
    key_value = shaped[1:]
    blocks_here = local_rows // BLK
    wide_count = lax.axis_size("wide")
    position = lax.axis_index("wide")
    scale_value = 1.0 / math.sqrt(HDIM)
    query_ids = block_tokens(
        lax.dynamic_slice_in_dim(block_image, position * blocks_here, blocks_here), BLK
    )

    def source_ids(source):
        inside = (source >= 0) & (source < wide_count)
        clipped = jnp.clip(source, 0, wide_count - 1)
        found_ids = block_tokens(
            lax.dynamic_slice_in_dim(block_image, clipped * blocks_here, blocks_here), BLK
        )
        return jnp.where(inside, found_ids, -2)

    totals = (
        jnp.zeros((local_rows, head_count, HDIM), jnp.float32),
        jnp.full((local_rows, head_count), neg_large, jnp.float32),
        jnp.zeros((local_rows, head_count), jnp.float32),
    )
    reach_steps = min(wide_count - 1, (MOST + blocks_here - 2) // blocks_here)
    totals = fold_keys(
        totals, query_ids, query_head, key_value[0], key_value[1], query_ids, scale_value
    )
    upward = key_value
    downward = key_value
    for distance in range(1, reach_steps + 1):
        upward = from_behind(upward, "wide", 1)
        totals = fold_keys(
            totals,
            query_ids,
            query_head,
            upward[0],
            upward[1],
            source_ids(position - distance),
            scale_value,
        )
        downward = from_behind(downward, "wide", -1)
        totals = fold_keys(
            totals,
            query_ids,
            query_head,
            downward[0],
            downward[1],
            source_ids(position + distance),
            scale_value,
        )
    acc_out, run_max, run_den = totals
    result = (
        (acc_out / run_den[..., None]).astype(jnp.bfloat16).reshape(local_rows, head_count * HDIM)
    )
    restored = lax.all_to_all(result, "grp", split_axis=0, concat_axis=1, tiled=True)
    return restored


def solution(mesh):
    return jax.shard_map(
        body,
        mesh=mesh,
        in_specs=(
            P(("wide", "grp"), None),
            P(("wide", "grp"), None),
            P(("wide", "grp"), None),
            P(),
        ),
        out_specs=P(("wide", "grp"), None),
        check_vma=False,
    )
```

profile of v0, /device:TPU:6, one launch (start us, length us, event | category | flops | bytes accessed | tf_op | source)
XLA Modules:
  0.0 92.8 jit_solution(2547221350390217727)
XLA Ops:
  0.0 0.0 copy-start
  0.0 1.3 %pad_maximum_fusion = bf16[3,128,1280]{2,1,0:T(8,128)(2,1)S(1)} fusion(bf16[1,128,1280]{2,1,0:T(8,128)(2,1)} %bitcast.190, bf16[1,128,1280]{2,1,0:T(8,128)(2,1)} %bitcast.191, bf16[1,128,1280]{2,1,0:T(8,128)(2,1)} %bitcast.192), kind=kLoop, calls=%fused_computation.51 | loop fusion | flops 983040 | bytes 1966080 | tf_op jit(solution)/shard_map/stack | solution.py:51
  1.3 2.2 %copy.41 = bf16[3,128,1280]{1,0,2:T(4,128)(2,1)} copy(bf16[3,128,1280]{2,1,0:T(8,128)(2,1)S(1)} %pad_maximum_fusion) | data formatting | bytes 1966080 | tf_op jit(solution)/shard_map/stack | solution.py:51
  3.5 4.5 %all-to-all-start = ((bf16[3,128,1280]{1,0,2:T(4,128)(2,1)}), bf16[3,128,1280]{1,0,2:T(4,128)(2,1)S(1)}, u32[]{:S(2)}, u32[]{:S(2)}) async-start(bf16[3,128,1280]{1,0,2:T(4,128)(2,1)} %copy.41), calls=%async_computation | async-start | bytes 2621440 | tf_op jit(solution)/shard_map/all_to_all | solution.py:52
  7.9 0.0 copy-done
  7.9 0.1 broadcast_select_fusion.3
  8.0 0.1 broadcast_bitcast_fusion.4
  8.1 0.1 broadcast_bitcast_fusion.2
  8.2 0.1 broadcast_bitcast_fusion
  8.2 17.6 %all-to-all-done = bf16[3,128,1280]{1,0,2:T(4,128)(2,1)S(1)} async-done(((bf16[3,128,1280]{1,0,2:T(4,128)(2,1)}), bf16[3,128,1280]{1,0,2:T(4,128)(2,1)S(1)}, u32[]{:S(2)}, u32[]{:S(2)}) %all-to-all-start) | async-done | bytes 983072 | tf_op jit(solution)/shard_map/all_to_all | solution.py:52
  25.8 0.1 copy.42
  26.0 0.5 copy.47
  26.6 1.1 %slice.48 = bf16[2,512,4,80]{1,3,2,0:T(8,128)(2,1)} reshape(bf16[2,4,128,320]{2,1,3,0:T(4,128)(2,1)S(1)} %copy.47) | data formatting | bytes 1310720 | tf_op jit(solution)/shard_map/slice | solution.py:57
  27.6 9.9 %collective-permute-start.1 = (bf16[2,512,4,80]{1,3,2,0:T(8,128)(2,1)}, bf16[2,512,4,80]{1,3,2,0:T(8,128)(2,1)}, u32[]{:S(2)}, u32[]{:S(2)}) collective-permute-start(bf16[2,512,4,80]{1,3,2,0:T(8,128)(2,1)} %slice.48), channel_id=1, source_target_pairs={{4,0},{8,4},{12,8},{16,12},{20,16},{24,20},{28,24},{32,28},{36,32}... | collective-permute-start | bytes 1966088 | tf_op jit(solution)/shard_map/ppermute | solution.py:19
  37.6 1.9 %collective-permute-start = (bf16[2,512,4,80]{1,3,2,0:T(8,128)(2,1)}, bf16[2,512,4,80]{1,3,2,0:T(8,128)(2,1)}, u32[]{:S(2)}, u32[]{:S(2)}) collective-permute-start(bf16[2,512,4,80]{1,3,2,0:T(8,128)(2,1)} %slice.48), channel_id=1, source_target_pairs={{0,4},{4,8},{8,12},{12,16},{16,20},{20,24},{24,28},{28,32},{32,36}... | collective-permute-start | bytes 1966088 | tf_op jit(solution)/shard_map/ppermute | solution.py:19
  39.5 0.9 broadcast_compare_fusion.4
  40.4 0.1 fusion.100
  40.4 0.3 copy.45
  40.7 0.1 squeeze.35
  40.8 0.3 copy.44
  41.1 0.1 squeeze.34
  41.2 0.3 copy.43
  41.5 0.1 squeeze.33
  41.6 1.0 %fusion = (f32[512,4]{0,1:T(4,128)S(1)}, f32[4,512,512]{2,1,0:T(8,128)S(1)}) fusion(pred[512,512]{0,1:T(8,128)(4,1)S(1)} %get-tuple-element.19, bf16[512,4,80]{0,2,1:T(8,128)(2,1)S(1)} %squeeze.33, bf16[512,4,80]{0,2,1:T(8,128)(2,1)S(1)} %squeeze.34), kind=kOutput, calls=%fused_computation.10 | convolution fusion | flops 170915840 | bytes 5120000 | tf_op jit(solution)/shard_map/qhd,khd->qhk/dot_general | solution.py:30
  42.6 3.4 %collective-permute-done.1 = bf16[2,512,4,80]{1,3,2,0:T(8,128)(2,1)} collective-permute-done((bf16[2,512,4,80]{1,3,2,0:T(8,128)(2,1)}, bf16[2,512,4,80]{1,3,2,0:T(8,128)(2,1)}, u32[]{:S(2)}, u32[]{:S(2)}) %collective-permute-start.1) | collective-permute-done | bytes 655392 | tf_op jit(solution)/shard_map/ppermute | solution.py:19
  46.0 5.9 %collective-permute-start.3 = (bf16[2,512,4,80]{1,3,2,0:T(8,128)(2,1)}, bf16[2,512,4,80]{1,3,2,0:T(8,128)(2,1)S(1)}, u32[]{:S(2)}, u32[]{:S(2)}) collective-permute-start(bf16[2,512,4,80]{1,3,2,0:T(8,128)(2,1)} %collective-permute-done.1), channel_id=1, source_target_pairs={{4,0},{8,4},{12,8},{16,12},{20,16},{24,20},{28,24},{32,28},{36,32}... | collective-permute-start | bytes 1966088 | tf_op jit(solution)/shard_map/ppermute | solution.py:19
  51.9 0.0 collective-permute-done
  51.9 2.1 %collective-permute-start.2 = (bf16[2,512,4,80]{1,3,2,0:T(8,128)(2,1)}, bf16[2,512,4,80]{1,3,2,0:T(8,128)(2,1)S(1)}, u32[]{:S(2)}, u32[]{:S(2)}) collective-permute-start(bf16[2,512,4,80]{1,3,2,0:T(8,128)(2,1)} %collective-permute-done), channel_id=1, source_target_pairs={{0,4},{4,8},{8,12},{12,16},{16,20},{20,24},{24,28},{28,32},{32,36}... | collective-permute-start | bytes 1966088 | tf_op jit(solution)/shard_map/ppermute | solution.py:19
  54.0 1.9 %fusion.2 = (f32[512,4]{0,1:T(4,128)S(1)}, f32[4,512,512]{2,1,0:T(8,128)S(1)}) fusion(pred[512,512]{0,1:T(8,128)(4,1)S(1)} %get-tuple-element.20, bf16[512,4,80]{0,2,1:T(8,128)(2,1)S(1)} %squeeze.34, bf16[2,512,4,80]{1,3,2,0:T(8,128)(2,1)} %collective-permute-done.1), kind=kOutput, calls=%fused_computation.12 | convolution fusion | flops 170915840 | bytes 5120000 | tf_op jit(solution)/shard_map/qhd,khd->qhk/dot_general | solution.py:30
  55.9 1.9 %fusion.1 = (f32[512,4]{0,1:T(4,128)S(1)}, f32[4,512,512]{2,1,0:T(8,128)S(1)}) fusion(pred[512,512]{0,1:T(8,128)(4,1)S(1)} %get-tuple-element.23, bf16[512,4,80]{0,2,1:T(8,128)(2,1)S(1)} %squeeze.34, bf16[2,512,4,80]{1,3,2,0:T(8,128)(2,1)} %collective-permute-done), kind=kOutput, calls=%fused_computation.11 | convolution fusion | flops 170915840 | bytes 5120000 | tf_op jit(solution)/shard_map/qhd,khd->qhk/dot_general | solution.py:30
  57.9 8.2 %collective-permute-done.2 = bf16[2,512,4,80]{1,3,2,0:T(8,128)(2,1)S(1)} collective-permute-done((bf16[2,512,4,80]{1,3,2,0:T(8,128)(2,1)}, bf16[2,512,4,80]{1,3,2,0:T(8,128)(2,1)S(1)}, u32[]{:S(2)}, u32[]{:S(2)}) %collective-permute-start.2) | collective-permute-done | bytes 655392 | tf_op jit(solution)/shard_map/ppermute | solution.py:19
  66.1 1.0 %fusion.3 = (f32[512,4]{0,1:T(4,128)S(1)}, f32[4,512,512]{2,1,0:T(8,128)S(1)}) fusion(pred[512,512]{0,1:T(8,128)(4,1)S(1)} %get-tuple-element.21, bf16[512,4,80]{0,2,1:T(8,128)(2,1)S(1)} %squeeze.34, bf16[2,512,4,80]{1,3,2,0:T(8,128)(2,1)S(1)} %collective-permute-done.2), kind=kOutput, calls=%fused_computation.13 | convolution fusion | flops 170915840 | bytes 5120000 | tf_op jit(solution)/shard_map/qhd,khd->qhk/dot_general | solution.py:30
  67.1 0.0 collective-permute-done.3
  67.1 1.0 %fusion.4 = (f32[512,4]{0,1:T(4,128)S(1)}, f32[4,512,512]{2,1,0:T(8,128)S(1)}) fusion(pred[512,512]{0,1:T(8,128)(4,1)S(1)} %get-tuple-element.22, bf16[512,4,80]{0,2,1:T(8,128)(2,1)S(1)} %squeeze.34, bf16[2,512,4,80]{1,3,2,0:T(8,128)(2,1)S(1)} %collective-permute-done.3), kind=kOutput, calls=%fused_computation.14 | convolution fusion | flops 170915840 | bytes 5120000 | tf_op jit(solution)/shard_map/qhd,khd->qhk/dot_general | solution.py:30
  68.1 1.0 %fusion.13 = f32[512,4]{0,1:T(4,128)S(1)} fusion(f32[4,512,512]{2,1,0:T(8,128)S(1)} %get-tuple-element.30, f32[512,4]{0,1:T(4,128)S(1)} %get-tuple-element.10, pred[512,512]{0,1:T(8,128)(4,1)S(1)} %get-tuple-element.22), kind=kLoop, calls=%fused_computation.23 | loop fusion | flops 5240832 | bytes 4472832 | tf_op jit(solution)/shard_map/reduce_sum | solution.py:37
  69.1 1.1 %fusion.9 = f32[512,4]{0,1:T(4,128)S(1)} fusion(f32[4,512,512]{2,1,0:T(8,128)S(1)} %get-tuple-element.34, f32[512,4]{0,1:T(4,128)S(1)} %get-tuple-element.12, pred[512,512]{0,1:T(8,128)(4,1)S(1)} %get-tuple-element.20), kind=kLoop, calls=%fused_computation.19 | loop fusion | flops 5240832 | bytes 4472832 | tf_op jit(solution)/shard_map/reduce_sum | solution.py:37
  70.2 1.1 %fusion.5 = f32[512,4]{0,1:T(4,128)S(1)} fusion(f32[4,512,512]{2,1,0:T(8,128)S(1)} %get-tuple-element.38, f32[512,4]{0,1:T(4,128)S(1)} %get-tuple-element.18, pred[512,512]{0,1:T(8,128)(4,1)S(1)} %get-tuple-element.19), kind=kLoop, calls=%fused_computation.15 | loop fusion | flops 5240832 | bytes 4472832 | tf_op jit(solution)/shard_map/reduce_sum | solution.py:37
  71.3 1.1 %fusion.11 = f32[512,4]{0,1:T(4,128)S(1)} fusion(f32[4,512,512]{2,1,0:T(8,128)S(1)} %get-tuple-element.32, f32[512,4]{0,1:T(4,128)S(1)} %get-tuple-element.11, pred[512,512]{0,1:T(8,128)(4,1)S(1)} %get-tuple-element.21), kind=kLoop, calls=%fused_computation.21 | loop fusion | flops 5240832 | bytes 4472832 | tf_op jit(solution)/shard_map/reduce_sum | solution.py:37
  72.3 1.0 %fusion.7 = f32[512,4]{0,1:T(4,128)S(1)} fusion(f32[4,512,512]{2,1,0:T(8,128)S(1)} %get-tuple-element.36, f32[512,4]{0,1:T(4,128)S(1)} %get-tuple-element.13, pred[512,512]{0,1:T(8,128)(4,1)S(1)} %get-tuple-element.23), kind=kLoop, calls=%fused_computation.17 | loop fusion | flops 5240832 | bytes 4472832 | tf_op jit(solution)/shard_map/reduce_sum | solution.py:37
  73.4 1.3 %fusion.69 = f32[512,4,80]{0,2,1:T(8,128)S(1)} fusion(bf16[512,4,80]{0,2,1:T(8,128)(2,1)S(1)} %squeeze.35, f32[4,512,512]{2,1,0:T(8,128)S(1)} %get-tuple-element.38, f32[512,4]{0,1:T(4,128)S(1)} %get-tuple-element.18, pred[512,512]{0,1:T(8,128)(4,1)S(1)} %get-tuple-element.19, f32[512,4]{0,1:T(4,128)S(1)} %get-tuple-element.9, ...), kind=kOutput, calls=%fused_computation.48 | convolution fusion | flops 173342720 | bytes 5464064 | tf_op jit(solution)/shard_map/qhk,khd->qhd/dot_general | solution.py:38
  74.7 1.4 %fusion.42 = f32[512,4,80]{0,2,1:T(8,128)S(1)} fusion(f32[4,512,512]{2,1,0:T(8,128)S(1)} %get-tuple-element.30, f32[512,4]{0,1:T(4,128)S(1)} %get-tuple-element.10, pred[512,512]{0,1:T(8,128)(4,1)S(1)} %get-tuple-element.22, bf16[2,512,4,80]{1,3,2,0:T(8,128)(2,1)S(1)} %collective-permute-done.3), kind=kOutput, calls=%fused_computation.39 | convolution fusion | flops 173015040 | bytes 5447680 | tf_op jit(solution)/shard_map/qhk,khd->qhd/dot_general | solution.py:38
  76.1 2.5 %fusion.36 = f32[512,4,80]{0,2,1:T(8,128)S(1)} fusion(f32[4,512,512]{2,1,0:T(8,128)S(1)} %get-tuple-element.34, f32[512,4]{0,1:T(4,128)S(1)} %get-tuple-element.12, pred[512,512]{0,1:T(8,128)(4,1)S(1)} %get-tuple-element.20, bf16[2,512,4,80]{1,3,2,0:T(8,128)(2,1)} %collective-permute-done.1), kind=kOutput, calls=%fused_computation.37 | convolution fusion | flops 173015040 | bytes 5447680 | tf_op jit(solution)/shard_map/qhk,khd->qhd/dot_general | solution.py:38
  78.6 2.3 %fusion.63 = f32[512,4,80]{0,2,1:T(8,128)S(1)} fusion(f32[512,4,80]{0,2,1:T(8,128)S(1)} %fusion.36, f32[512,4,80]{0,2,1:T(8,128)S(1)} %fusion.69, f32[4,512,512]{2,1,0:T(8,128)S(1)} %get-tuple-element.36, f32[512,4]{0,1:T(4,128)S(1)} %get-tuple-element.13, pred[512,512]{0,1:T(8,128)(4,1)S(1)} %get-tuple-element.23, ...), kind=kOutput, calls=%fused_computation.46 | convolution fusion | flops 173670400 | bytes 6774784 | tf_op jit(solution)/shard_map/qhk,khd->qhd/dot_general | solution.py:38
  80.9 1.4 %fusion.75 = bf16[512,4,80]{0,2,1:T(8,128)(2,1)S(1)} fusion(f32[512,4,80]{0,2,1:T(8,128)S(1)} %fusion.42, f32[512,4,80]{0,2,1:T(8,128)S(1)} %fusion.63, f32[4,512,512]{2,1,0:T(8,128)S(1)} %get-tuple-element.32, f32[512,4]{0,1:T(4,128)S(1)} %get-tuple-element.11, pred[512,512]{0,1:T(8,128)(4,1)S(1)} %get-tuple-element.21, ...), kind=kOutput, calls=%fused_computation.50 | convolution fusion | flops 173834240 | bytes 6447104 | tf_op jit(solution)/shard_map/qhk,khd->qhd/dot_general | solution.py:38
  82.3 0.1 all_to_all.28
  82.5 9.4 %all_to_all.34 = bf16[4,128,320]{1,2,0:T(8,128)(2,1)S(1)} all-to-all(bf16[4,128,320]{1,2,0:T(8,128)(2,1)S(1)} %copy.52), channel_id=1, replica_groups=mesh['wide'=128,'grp'=4] {'grp'}, dimensions={0} | all-to-all | bytes 655360 | tf_op jit(solution)/shard_map/all_to_all | solution.py:110
  91.9 0.9 copy.53
  (4 shorter events, 0.1 us)
Async XLA Ops:
  0.0 7.9 %copy-start = (s32[512]{0:T(512)S(1)}, s32[512]{0:T(512)}, u32[]{:S(2)}) copy-start(s32[512]{0:T(512)} %param.7) | copy-start | bytes 6148
  3.5 22.4 %all-to-all-start = ((bf16[3,128,1280]{1,0,2:T(4,128)(2,1)}), bf16[3,128,1280]{1,0,2:T(4,128)(2,1)S(1)}, u32[]{:S(2)}, u32[]{:S(2)}) async-start(bf16[3,128,1280]{1,0,2:T(4,128)(2,1)} %copy.41), calls=%async_computation | async-start | bytes 2621440 | tf_op jit(solution)/shard_map/all_to_all | solution.py:52
  27.6 18.3 %collective-permute-start.1 = (bf16[2,512,4,80]{1,3,2,0:T(8,128)(2,1)}, bf16[2,512,4,80]{1,3,2,0:T(8,128)(2,1)}, u32[]{:S(2)}, u32[]{:S(2)}) collective-permute-start(bf16[2,512,4,80]{1,3,2,0:T(8,128)(2,1)} %slice.48), channel_id=1, source_target_pairs={{4,0},{8,4},{12,8},{16,12},{20,16},{24,20},{28,24},{32,28},{36,32}... | collective-permute-start | bytes 1966088 | tf_op jit(solution)/shard_map/ppermute | solution.py:19
  37.6 14.3 %collective-permute-start = (bf16[2,512,4,80]{1,3,2,0:T(8,128)(2,1)}, bf16[2,512,4,80]{1,3,2,0:T(8,128)(2,1)}, u32[]{:S(2)}, u32[]{:S(2)}) collective-permute-start(bf16[2,512,4,80]{1,3,2,0:T(8,128)(2,1)} %slice.48), channel_id=1, source_target_pairs={{0,4},{4,8},{8,12},{12,16},{16,20},{20,24},{24,28},{28,32},{32,36}... | collective-permute-start | bytes 1966088 | tf_op jit(solution)/shard_map/ppermute | solution.py:19
  46.0 21.1 %collective-permute-start.3 = (bf16[2,512,4,80]{1,3,2,0:T(8,128)(2,1)}, bf16[2,512,4,80]{1,3,2,0:T(8,128)(2,1)S(1)}, u32[]{:S(2)}, u32[]{:S(2)}) collective-permute-start(bf16[2,512,4,80]{1,3,2,0:T(8,128)(2,1)} %collective-permute-done.1), channel_id=1, source_target_pairs={{4,0},{8,4},{12,8},{16,12},{20,16},{24,20},{28,24},{32,28},{36,32}... | collective-permute-start | bytes 1966088 | tf_op jit(solution)/shard_map/ppermute | solution.py:19
  51.9 14.2 %collective-permute-start.2 = (bf16[2,512,4,80]{1,3,2,0:T(8,128)(2,1)}, bf16[2,512,4,80]{1,3,2,0:T(8,128)(2,1)S(1)}, u32[]{:S(2)}, u32[]{:S(2)}) collective-permute-start(bf16[2,512,4,80]{1,3,2,0:T(8,128)(2,1)} %collective-permute-done), channel_id=1, source_target_pairs={{0,4},{4,8},{8,12},{12,16},{16,20},{20,24},{24,28},{28,32},{32,36}... | collective-permute-start | bytes 1966088 | tf_op jit(solution)/shard_map/ppermute | solution.py:19
where the time goes:
time: 93.2 us; the launch traced here: 92.8 us
  waiting for transfers between devices  29.2 us (31%)
  starting transfers between devices  24.3 us (26%)
  matrix products  15.7 us (17%)
  blocking collectives  9.4 us (10%)
  other arithmetic  7.57 us (8%)
  local copies, waits for them, and re-layouts  6.42 us (7%)
    ppermute x4, starting transfers between devices, from_behind(): lax.ppermute(value, axis, [(source, source + steps) for source in range(l...  19.8 us
    all_to_all x1, waiting for transfers between devices, body(): lax.all_to_all(stacked, 'grp', split_axis=2, concat_axis=1, tiled=True)  17.6 us
    ppermute x4, waiting for transfers between devices, from_behind(): lax.ppermute(value, axis, [(source, source + steps) for source in range(l...  11.6 us
    all_to_all x1, blocking collectives, body(): lax.all_to_all(result, 'grp', split_axis=0, concat_axis=1, tiled=True)  9.4 us
    dot_general x5, matrix products, fold_tile(): jnp.einsum('qhk,khd->qhd', weights.astype(jnp.bfloat16), value_head, pref...  8.9 us
    dot_general x5, matrix products, fold_tile(): jnp.einsum('qhd,khd->qhk', query_head, key_head, preferred_element_type=j...  6.8 us
    reduce_sum x5, other arithmetic, fold_tile(): run_den = run_den * fading + jnp.sum(weights, axis=-1)  5.27 us
    all_to_all x1, starting transfers between devices, body(): lax.all_to_all(stacked, 'grp', split_axis=2, concat_axis=1, tiled=True)  4.46 us
  transfers between devices with their start and end apart: 5, of which 3 were waited for; matrix products, arithmetic and copies ran while one was open for 9% of the time, Pallas kernels for 0%

commit v1 on v0

v1 whole, which is shorter than its diff:
```python
import math

import jax
import jax.numpy as jnp
from jax import lax
from jax.experimental import pallas as pl
from jax.experimental.pallas import tpu as pltpu
from jax.sharding import PartitionSpec as P

HDIM = 80
BLK = 128
PER = 8
HEADS_HERE = 2
WIDTH = HEADS_HERE * HDIM
SCALE_LOG2 = math.log2(math.e) / math.sqrt(HDIM)
FAR = 1e30
VMEM = pl.BlockSpec(memory_space=pltpu.VMEM)
SMEM = pl.BlockSpec(memory_space=pltpu.SMEM)
LIMIT = pltpu.CompilerParams(vmem_limit_bytes=24 * 1024 * 1024)
F32 = jnp.float32
BF16 = jnp.bfloat16


def split_kernel(*refs):
    out_ref = refs[-1]
    for place, ref in enumerate(refs[:-1]):
        turned = ref[...].T
        for part in range(PER):
            out_ref[part, place * WIDTH : (place + 1) * WIDTH, :] = turned[part * WIDTH : (part + 1) * WIDTH, :]


def split_heads(*arrays):
    return pl.pallas_call(
        split_kernel,
        out_shape=jax.ShapeDtypeStruct((PER, WIDTH * len(arrays), BLK), BF16),
        in_specs=[VMEM] * len(arrays),
        out_specs=VMEM,
        compiler_params=LIMIT,
        name="split_heads",
    )(*arrays)


def join_kernel(in_ref, out_ref):
    out_ref[...] = in_ref[...].reshape(PER * WIDTH, BLK).T


def join_heads(parts):
    return pl.pallas_call(
        join_kernel,
        out_shape=jax.ShapeDtypeStruct((BLK, PER * WIDTH), BF16),
        in_specs=[VMEM],
        out_specs=VMEM,
        compiler_params=LIMIT,
        name="join_heads",
    )(parts)


def both_heads(query):
    row = lax.broadcasted_iota(jnp.int32, (WIDTH, BLK), 0)
    none = jnp.zeros_like(query)
    return jnp.concatenate((jnp.where(row < HDIM, query, none), jnp.where(row < HDIM, none, query)), axis=1)


def diagonal(total):
    return jnp.concatenate((total[:HDIM, :BLK], total[HDIM:, BLK:]), axis=0)


def per_row(stat):
    return jnp.concatenate(
        (
            jnp.broadcast_to(stat[:, :BLK], (HDIM, BLK)),
            jnp.broadcast_to(stat[:, BLK:], (HDIM, BLK)),
        ),
        axis=0,
    )


def own_kernel(span_ref, kv_ref, q_ref, out_ref, acc_ref, max_ref, den_ref, keys, scores):
    for block in range(PER):
        keys[block * BLK : (block + 1) * BLK, :] = kv_ref[block, :WIDTH, :].T

    def one(i, carry):
        first, last = span_ref[0, i], span_ref[1, i]
        weights_in = both_heads(q_ref[i])
        top = jnp.full((1, 2 * BLK), -FAR, F32)
        for j in range(PER):
            rows = slice(j * BLK, (j + 1) * BLK)
            found = jnp.dot(keys[rows, :], weights_in, preferred_element_type=F32)
            scores[rows, :] = found
            inside = (j >= first) & (j < last)
            top = jnp.maximum(top, jnp.where(inside, jnp.max(found, axis=0, keepdims=True), -FAR))
        shift = top * SCALE_LOG2
        total = jnp.zeros((WIDTH, 2 * BLK), F32)
        den = jnp.zeros((1, 2 * BLK), F32)
        for j in range(PER):
            rows = slice(j * BLK, (j + 1) * BLK)
            inside = (j >= first) & (j < last)
            here = jnp.where(inside, shift, FAR)
            weights = jnp.exp2(scores[rows, :] * SCALE_LOG2 - here)
            den += jnp.sum(weights, axis=0, keepdims=True)
            total += jnp.dot(kv_ref[j, WIDTH:, :], weights.astype(BF16), preferred_element_type=F32)
        acc = diagonal(total)
        acc_ref[i] = acc
        max_ref[i] = top
        den_ref[i] = den
        out_ref[i] = (acc / per_row(den)).astype(BF16)
        return carry

    lax.fori_loop(0, PER, one, 0)


def own_part(span, kv, q):
    return pl.pallas_call(
        own_kernel,
        out_shape=(
            jax.ShapeDtypeStruct((PER, WIDTH, BLK), BF16),
            jax.ShapeDtypeStruct((PER, WIDTH, BLK), F32),
            jax.ShapeDtypeStruct((PER, 1, 2 * BLK), F32),
            jax.ShapeDtypeStruct((PER, 1, 2 * BLK), F32),
        ),
        in_specs=[SMEM, VMEM, VMEM],
        out_specs=(VMEM,) * 4,
        scratch_shapes=[pltpu.VMEM((PER * BLK, WIDTH), BF16), pltpu.VMEM((PER * BLK, 2 * BLK), F32)],
        compiler_params=LIMIT,
        cost_estimate=pl.CostEstimate(flops=4_000_000_000, bytes_accessed=4_000_000, transcendentals=2_000_000),
        name="own_part",
    )(span, kv, q)


def halo_kernel(span_ref, below_ref, above_ref, q_ref, start_ref, acc_ref, max_ref, den_ref, out_ref, keys):
    out_ref[...] = start_ref[...]

    def reach(kv_ref, row, first_query, last_query):
        low, high = span_ref[row, 0], span_ref[row, 1]

        def turn(j, carry):
            keys[pl.ds(pl.multiple_of(j * BLK, BLK), BLK), :] = kv_ref[j, :WIDTH, :].T
            return carry

        lax.fori_loop(low, high, turn, 0)

        def one(i, carry):
            weights_in = both_heads(q_ref[i])
            start = (acc_ref[i], max_ref[i], den_ref[i])

            def fold(j, state):
                acc, top, den = state
                found = jnp.dot(
                    keys[pl.ds(pl.multiple_of(j * BLK, BLK), BLK), :], weights_in, preferred_element_type=F32
                )
                new = jnp.maximum(top, jnp.max(found, axis=0, keepdims=True))
                fade = jnp.exp2((top - new) * SCALE_LOG2)
                weights = jnp.exp2(found * SCALE_LOG2 - new * SCALE_LOG2)
                den = den * fade + jnp.sum(weights, axis=0, keepdims=True)
                more = jnp.dot(kv_ref[j, WIDTH:, :], weights.astype(BF16), preferred_element_type=F32)
                return acc * per_row(fade) + diagonal(more), new, den

            acc, top, den = lax.fori_loop(low, high, fold, start)
            out_ref[i] = (acc / per_row(den)).astype(BF16)
            return carry

        lax.fori_loop(first_query, last_query, one, 0)

    reach(below_ref, 2, 0, span_ref[2, 2])
    reach(above_ref, 3, span_ref[3, 2], PER)


def halo_part(span, below, above, q, start, acc, top, den):
    return pl.pallas_call(
        halo_kernel,
        out_shape=jax.ShapeDtypeStruct((PER, WIDTH, BLK), BF16),
        in_specs=[SMEM] + [VMEM] * 7,
        out_specs=VMEM,
        scratch_shapes=[pltpu.VMEM((PER * BLK, WIDTH), BF16)],
        input_output_aliases={4: 0},
        compiler_params=LIMIT,
        cost_estimate=pl.CostEstimate(flops=1_000_000_000, bytes_accessed=4_000_000, transcendentals=1_000_000),
        name="halo_part",
    )(span, below, above, q, start, acc, top, den)


def shifted(value, steps):
    count = lax.axis_size("sup")
    pairs = [(i, i + steps) for i in range(count) if 0 <= i + steps < count]
    return lax.ppermute(value, "sup", pairs)


def spans(block_image):
    sup = lax.axis_index("sup")
    here = lax.dynamic_slice_in_dim(block_image, sup * PER, PER)
    low = jnp.sum((block_image[None, :] < here[:, None]).astype(jnp.int32), axis=1) - sup * PER
    high = jnp.sum((block_image[None, :] <= here[:, None]).astype(jnp.int32), axis=1) - sup * PER
    zeros = jnp.zeros((PER,), jnp.int32)
    below = zeros.at[0].set(PER + jnp.minimum(low[0], 0)).at[1].set(PER)
    below = below.at[2].set(jnp.where(low[0] < 0, jnp.sum((low < 0).astype(jnp.int32)), 0))
    above = zeros.at[1].set(jnp.maximum(high[PER - 1] - PER, 0))
    above = above.at[2].set(PER - jnp.sum((high > PER).astype(jnp.int32)))
    return jnp.stack((jnp.maximum(low, 0), jnp.minimum(high, PER), below, above))


def body(query_rows, key_rows, value_rows, block_image):
    group = ("core", "grp")
    span = spans(block_image)
    kv = lax.all_to_all(split_heads(key_rows, value_rows), group, 0, 0, tiled=True)
    q = split_heads(query_rows)
    kv, q = lax.optimization_barrier((kv, q))
    below = shifted(kv, 1)
    above = shifted(kv, -1)
    q = lax.all_to_all(q, group, 0, 0, tiled=True)
    start, acc, top, den = own_part(span, kv, q)
    result = halo_part(span, below, above, q, start, acc, top, den)
    back = lax.all_to_all(result, group, 0, 0, tiled=True)
    return join_heads(back)


def solution(mesh):
    per_group = mesh.shape["grp"]
    cores = PER // per_group
    devices = mesh.devices.reshape(-1, cores, per_group)
    inner = jax.sharding.Mesh(devices, ("sup", "core", "grp"))
    rows = P(("sup", "core", "grp"), None)
    return jax.shard_map(
        body,
        mesh=inner,
        in_specs=(rows, rows, rows, P()),
        out_specs=rows,
        check_vma=False,
    )
```

time: 93.2 us -> 70.5 us (0.76)
  the two profiles are of different devices: /device:TPU:6 before, /device:TPU:5 now
where the time goes in v1:
time: 70.5 us; the launch traced here: 70 us
  starting transfers between devices  22.3 us (32%)
  Pallas kernels  17.1 us (24%)
  waiting for transfers between devices  12.3 us (17%)
  blocking collectives  11.2 us (16%)
  local copies, waits for them, and re-layouts  3.71 us (5%)
  between operations  2 us (3%)
  other arithmetic  1.51 us (2%)
    ppermute x2, starting transfers between devices, shifted(): return lax.ppermute(value, 'sup', pairs)  13 us
    all_to_all x1, blocking collectives, body(): back = lax.all_to_all(result, group, 0, 0, tiled=True)  11.2 us
    pallas_call x1, Pallas kernels, halo_part(): pl.pallas_call(halo_kernel, out_shape=jax.ShapeDtypeStruct((PER, WIDTH, B...  7.9 us
    pallas_call x1, Pallas kernels, own_part(): pl.pallas_call(own_kernel, out_shape=(jax.ShapeDtypeStruct((PER, WIDTH, B...  6.42 us
    all_to_all x1, waiting for transfers between devices, body(): lax.all_to_all(split_heads(key_rows, value_rows), group, 0, 0, tiled=True)  6.4 us
    all_to_all x1, waiting for transfers between devices, body(): q = lax.all_to_all(q, group, 0, 0, tiled=True)  5.85 us
    all_to_all x1, starting transfers between devices, body(): lax.all_to_all(split_heads(key_rows, value_rows), group, 0, 0, tiled=True)  5.27 us
    all_to_all x1, starting transfers between devices, body(): q = lax.all_to_all(q, group, 0, 0, tiled=True)  4.01 us
  transfers between devices with their start and end apart: 4, of which 2 were waited for; matrix products, arithmetic and copies ran while one was open for 4% of the time, Pallas kernels for 10%

profile of v1, /device:TPU:5, one launch (start us, length us, event | category | flops | bytes accessed | tf_op | source)
XLA Modules:
  0.0 70.0 jit_solution(1077898459265556518)
XLA Ops:
  0.0 0.0 copy-start
  0.0 1.0 %copy-done = bf16[128,1280]{1,0:T(8,128)(2,1)S(1)} copy-done((bf16[128,1280]{1,0:T(8,128)(2,1)S(1)}, bf16[128,1280]{1,0:T(8,128)(2,1)}, u32[]{:S(2)}) %copy-start) | copy-done | bytes 327704
  1.0 0.0 copy-start.1
  1.0 1.0 %copy-done.1 = bf16[128,1280]{1,0:T(8,128)(2,1)S(1)} copy-done((bf16[128,1280]{1,0:T(8,128)(2,1)S(1)}, bf16[128,1280]{1,0:T(8,128)(2,1)}, u32[]{:S(2)}) %copy-start.1) | copy-done | bytes 327704
  1.9 1.1 %split_heads.2 = bf16[8,320,128]{2,1,0:T(8,128)(2,1)} custom-call(bf16[128,1280]{1,0:T(8,128)(2,1)S(1)} %copy-done, bf16[128,1280]{1,0:T(8,128)(2,1)S(1)} %copy-done.1), custom_call_target="tpu_custom_call" | custom-call | tf_op jit(solution)/shard_map/split_heads/pallas_call | solution.py:33
  3.0 0.0 copy-start.2
  3.0 5.3 %all-to-all-start = ((bf16[8,320,128]{2,1,0:T(8,128)(2,1)}), bf16[8,320,128]{2,1,0:T(8,128)(2,1)S(1)}, u32[]{:S(2)}, u32[]{:S(2)}) async-start(bf16[8,320,128]{2,1,0:T(8,128)(2,1)} %split_heads.2), calls=%async_computation | async-start | bytes 1310720 | tf_op jit(solution)/shard_map/all_to_all | solution.py:204
  8.3 0.0 copy-start.3
  8.3 0.7 copy-done.3
  9.0 0.1 dynamic_slice.3
  9.0 0.2 convert_reduce_fusion.1
  9.2 0.6 slice.56
  9.9 0.0 copy-done.2
  9.9 0.9 %split_heads.3 = bf16[8,160,128]{2,1,0:T(8,128)(2,1)} custom-call(bf16[128,1280]{1,0:T(8,128)(2,1)S(1)} %copy-done.2), custom_call_target="tpu_custom_call" | custom-call | tf_op jit(solution)/shard_map/split_heads/pallas_call | solution.py:33
  11.4 0.6 fusion.1
  12.0 0.7 fusion
  12.7 6.4 %all-to-all-done.kv_ref = bf16[8,320,128]{2,1,0:T(8,128)(2,1)S(1)} async-done(((bf16[8,320,128]{2,1,0:T(8,128)(2,1)}), bf16[8,320,128]{2,1,0:T(8,128)(2,1)S(1)}, u32[]{:S(2)}, u32[]{:S(2)}) %all-to-all-start) | async-done | bytes 655392 | tf_op jit(solution)/shard_map/all_to_all | solution.py:204
  19.1 11.1 %collective-permute-start.1 = (bf16[8,320,128]{2,1,0:T(8,128)(2,1)S(1)}, bf16[8,320,128]{2,1,0:T(8,128)(2,1)S(1)}, u32[]{:S(2)}, u32[]{:S(2)}) collective-permute-start(bf16[8,320,128]{2,1,0:T(8,128)(2,1)S(1)} %all-to-all-done.kv_ref), channel_id=1, source_target_pairs={{8,0},{16,8},{24,16},{32,24},{40,32},{48,40},{56,48},{64,56},{72,6... | collective-permute-start | bytes 1966088 | tf_op jit(solution)/shard_map/ppermute | solution.py:185
  30.2 1.9 %collective-permute-start = (bf16[8,320,128]{2,1,0:T(8,128)(2,1)S(1)}, bf16[8,320,128]{2,1,0:T(8,128)(2,1)S(1)}, u32[]{:S(2)}, u32[]{:S(2)}) collective-permute-start(bf16[8,320,128]{2,1,0:T(8,128)(2,1)S(1)} %all-to-all-done.kv_ref), channel_id=1, source_target_pairs={{0,8},{8,16},{16,24},{24,32},{32,40},{40,48},{48,56},{56,64},{64,7... | collective-permute-start | bytes 1966088 | tf_op jit(solution)/shard_map/ppermute | solution.py:185
  32.1 4.0 %all-to-all-start.1 = ((bf16[8,160,128]{2,1,0:T(8,128)(2,1)}), bf16[8,160,128]{2,1,0:T(8,128)(2,1)S(1)}, u32[]{:S(2)}, u32[]{:S(2)}) async-start(bf16[8,160,128]{2,1,0:T(8,128)(2,1)} %split_heads.3), calls=%async_computation.1 | async-start | bytes 655360 | tf_op jit(solution)/shard_map/all_to_all | solution.py:209
  36.1 0.1 pad_bitcast_fusion
  37.5 0.1 scatter.24
  37.6 0.1 scatter.19
  37.7 0.1 scatter.20
  37.8 5.9 %all-to-all-done.1.q_ref = bf16[8,160,128]{2,1,0:T(8,128)(2,1)S(1)} async-done(((bf16[8,160,128]{2,1,0:T(8,128)(2,1)}), bf16[8,160,128]{2,1,0:T(8,128)(2,1)S(1)}, u32[]{:S(2)}, u32[]{:S(2)}) %all-to-all-start.1) | async-done | bytes 327712 | tf_op jit(solution)/shard_map/all_to_all | solution.py:209
  43.7 6.4 %own_part.1 = (bf16[8,160,128]{2,1,0:T(8,128)(2,1)S(1)}, f32[8,160,128]{2,1,0:T(8,128)S(1)}, f32[8,1,256]{2,1,0:T(1,128)S(1)}, f32[8,1,256]{2,1,0:T(1,128)S(1)}) custom-call(s32[4,8]{1,0:T(4,128)S(1)} %pad_add_fusion.span_ref, bf16[8,320,128]{2,1,0:T(8,128)(2,1)S(1)} %all-to-all-done.kv_ref, bf16[8,160,128]{2,1,0:T(8,128)(2,1)S(1)} %all-to-all-done.1.q_ref), custom_call_target="tpu_custom_call" | custom-call | flops 4000000000 | bytes 4000000 | tf_op jit(solution)/shard_map/own_part/pallas_call | solution.py:113
  50.1 0.0 collective-permute-done.1.above_ref
  50.1 0.0 collective-permute-done.below_ref
  50.1 7.9 %halo_part.1 = bf16[8,160,128]{2,1,0:T(8,128)(2,1)S(1)} custom-call(s32[4,8]{1,0:T(4,128)S(1)} %pad_add_fusion.span_ref, bf16[8,320,128]{2,1,0:T(8,128)(2,1)S(1)} %collective-permute-done.below_ref, bf16[8,320,128]{2,1,0:T(8,128)(2,1)S(1)} %collective-permute-done.1.above_ref, ...), custom_call_target="tpu_custom_call", output_to_operand_aliasing={{}: (4, {})} | custom-call | flops 1000000000 | bytes 4000000 | tf_op jit(solution)/shard_map/halo_part/pallas_call | solution.py:169
  58.0 11.2 %all_to_all.15.in_ref = bf16[8,160,128]{2,1,0:T(8,128)(2,1)S(1)} all-to-all(bf16[8,160,128]{2,1,0:T(8,128)(2,1)S(1)} %halo_part.1), channel_id=1, replica_groups=mesh['sup'=64,'core'=2,'grp'=4] {'core','grp'}, dimensions={0} | all-to-all | bytes 655360 | tf_op jit(solution)/shard_map/all_to_all | solution.py:212
  69.2 0.9 %join_heads.1 = bf16[128,1280]{1,0:T(8,128)(2,1)} custom-call(bf16[8,160,128]{2,1,0:T(8,128)(2,1)S(1)} %all_to_all.15.in_ref), custom_call_target="tpu_custom_call" | custom-call | tf_op jit(solution)/shard_map/join_heads/pallas_call | solution.py:48
  (3 shorter events, 0.0 us)
Async XLA Ops:
  0.0 1.0 %copy-start = (bf16[128,1280]{1,0:T(8,128)(2,1)S(1)}, bf16[128,1280]{1,0:T(8,128)(2,1)}, u32[]{:S(2)}) copy-start(bf16[128,1280]{1,0:T(8,128)(2,1)} %refs_0_.2) | copy-start | bytes 983044
  1.0 1.0 %copy-start.1 = (bf16[128,1280]{1,0:T(8,128)(2,1)S(1)}, bf16[128,1280]{1,0:T(8,128)(2,1)}, u32[]{:S(2)}) copy-start(bf16[128,1280]{1,0:T(8,128)(2,1)} %refs_1_.1) | copy-start | bytes 983044
  3.0 6.8 %copy-start.2 = (bf16[128,1280]{1,0:T(8,128)(2,1)S(1)}, bf16[128,1280]{1,0:T(8,128)(2,1)}, u32[]{:S(2)}) copy-start(bf16[128,1280]{1,0:T(8,128)(2,1)} %refs_0_.3) | copy-start | bytes 983044
  3.0 16.0 %all-to-all-start = ((bf16[8,320,128]{2,1,0:T(8,128)(2,1)}), bf16[8,320,128]{2,1,0:T(8,128)(2,1)S(1)}, u32[]{:S(2)}, u32[]{:S(2)}) async-start(bf16[8,320,128]{2,1,0:T(8,128)(2,1)} %split_heads.2), calls=%async_computation | async-start | bytes 1310720 | tf_op jit(solution)/shard_map/all_to_all | solution.py:204
  8.3 0.7 copy-start.3
  19.1 31.0 %collective-permute-start.1 = (bf16[8,320,128]{2,1,0:T(8,128)(2,1)S(1)}, bf16[8,320,128]{2,1,0:T(8,128)(2,1)S(1)}, u32[]{:S(2)}, u32[]{:S(2)}) collective-permute-start(bf16[8,320,128]{2,1,0:T(8,128)(2,1)S(1)} %all-to-all-done.kv_ref), channel_id=1, source_target_pairs={{8,0},{16,8},{24,16},{32,24},{40,32},{48,40},{56,48},{64,56},{72,6... | collective-permute-start | bytes 1966088 | tf_op jit(solution)/shard_map/ppermute | solution.py:185
  30.2 19.9 %collective-permute-start = (bf16[8,320,128]{2,1,0:T(8,128)(2,1)S(1)}, bf16[8,320,128]{2,1,0:T(8,128)(2,1)S(1)}, u32[]{:S(2)}, u32[]{:S(2)}) collective-permute-start(bf16[8,320,128]{2,1,0:T(8,128)(2,1)S(1)} %all-to-all-done.kv_ref), channel_id=1, source_target_pairs={{0,8},{8,16},{16,24},{24,32},{32,40},{40,48},{48,56},{56,64},{64,7... | collective-permute-start | bytes 1966088 | tf_op jit(solution)/shard_map/ppermute | solution.py:185
  32.1 11.6 %all-to-all-start.1 = ((bf16[8,160,128]{2,1,0:T(8,128)(2,1)}), bf16[8,160,128]{2,1,0:T(8,128)(2,1)S(1)}, u32[]{:S(2)}, u32[]{:S(2)}) async-start(bf16[8,160,128]{2,1,0:T(8,128)(2,1)} %split_heads.3), calls=%async_computation.1 | async-start | bytes 655360 | tf_op jit(solution)/shard_map/all_to_all | solution.py:209

commit v2 on v1

v2 whole, which is shorter than its diff:
```python
import functools
import math

import jax
import jax.numpy as jnp
from jax import lax
from jax.experimental import pallas as pl
from jax.experimental.pallas import tpu as pltpu
from jax.sharding import PartitionSpec as P

HDIM = 80
BLK = 128
PER = 8
HEADS_HERE = 2
WIDTH = HEADS_HERE * HDIM
TILES = PER * WIDTH // BLK
SCALE_LOG2 = math.log2(math.e) / math.sqrt(HDIM)
FAR = 1e30
SLOTS = 16
STEP = 4
VMEM = pl.BlockSpec(memory_space=pltpu.VMEM)
SMEM = pl.BlockSpec(memory_space=pltpu.SMEM)
HBM = pl.BlockSpec(memory_space=pltpu.HBM)
LIMIT = pltpu.CompilerParams(vmem_limit_bytes=24 * 1024 * 1024)
F32 = jnp.float32
BF16 = jnp.bfloat16


def cost(flops):
    return pl.CostEstimate(flops=flops, bytes_accessed=1_000_000, transcendentals=0)


def split_kernel(*refs):
    count = len(refs) - 3
    sources, out_ref, held, sems = refs[:count], refs[count], refs[count + 1], refs[count + 2]
    copies = [pltpu.make_async_copy(ref, held.at[place], sems.at[place]) for place, ref in enumerate(sources)]
    for copy in copies:
        copy.start()
    for place, copy in enumerate(copies):
        copy.wait()
        for tile in range(TILES):
            turned = held[place, :, tile * BLK : (tile + 1) * BLK].T
            first = tile * BLK
            while first < (tile + 1) * BLK:
                part, row = divmod(first, WIDTH)
                size = min((tile + 1) * BLK - first, WIDTH - row)
                skip = first - tile * BLK
                out_ref[part, place * WIDTH + row : place * WIDTH + row + size, :] = turned[skip : skip + size, :]
                first += size


def split_heads(*arrays):
    count = len(arrays)
    return pl.pallas_call(
        split_kernel,
        out_shape=jax.ShapeDtypeStruct((PER, WIDTH * count, BLK), BF16),
        in_specs=[HBM] * count,
        out_specs=VMEM,
        scratch_shapes=[pltpu.VMEM((count, BLK, PER * WIDTH), BF16), pltpu.SemaphoreType.DMA((count,))],
        cost_estimate=cost(500_000_000 * count),
        name="split_heads",
    )(*arrays)


def join_kernel(in_ref, out_ref):
    out_ref[...] = in_ref[...].reshape(PER * WIDTH, BLK).T


def join_heads(parts):
    return pl.pallas_call(
        join_kernel,
        out_shape=jax.ShapeDtypeStruct((BLK, PER * WIDTH), BF16),
        in_specs=[VMEM],
        out_specs=VMEM,
        compiler_params=LIMIT,
        name="join_heads",
    )(parts)


def both_heads(query):
    row = lax.broadcasted_iota(jnp.int32, (WIDTH, BLK), 0)
    none = jnp.zeros_like(query)
    return jnp.concatenate((jnp.where(row < HDIM, query, none), jnp.where(row < HDIM, none, query)), axis=1)


def diagonal(total):
    return jnp.concatenate((total[:HDIM, :BLK], total[HDIM:, BLK:]), axis=0)


def per_row(stat):
    return jnp.concatenate(
        (
            jnp.broadcast_to(stat[:, :BLK], (HDIM, BLK)),
            jnp.broadcast_to(stat[:, BLK:], (HDIM, BLK)),
        ),
        axis=0,
    )


def own_kernel(span_ref, qkv_ref, out_ref, acc_ref, max_ref, den_ref, keys, scores):
    for block in range(PER):
        keys[block * BLK : (block + 1) * BLK, :] = qkv_ref[block, WIDTH : 2 * WIDTH, :].T

    def one(i, carry):
        first, last = span_ref[0, i], span_ref[1, i]
        weights_in = both_heads(qkv_ref[i, :WIDTH, :])
        top = jnp.full((1, 2 * BLK), -FAR, F32)
        for j in range(PER):
            rows = slice(j * BLK, (j + 1) * BLK)
            found = jnp.dot(keys[rows, :], weights_in, preferred_element_type=F32)
            scores[rows, :] = found
            inside = (j >= first) & (j < last)
            top = jnp.maximum(top, jnp.where(inside, jnp.max(found, axis=0, keepdims=True), -FAR))
        shift = top * SCALE_LOG2
        total = jnp.zeros((WIDTH, 2 * BLK), F32)
        den = jnp.zeros((1, 2 * BLK), F32)
        for j in range(PER):
            rows = slice(j * BLK, (j + 1) * BLK)
            inside = (j >= first) & (j < last)
            here = jnp.where(inside, shift, FAR)
            weights = jnp.exp2(scores[rows, :] * SCALE_LOG2 - here)
            den += jnp.sum(weights, axis=0, keepdims=True)
            total += jnp.dot(qkv_ref[j, 2 * WIDTH :, :], weights.astype(BF16), preferred_element_type=F32)
        acc = diagonal(total)
        acc_ref[i] = acc
        max_ref[i] = top
        den_ref[i] = den
        out_ref[i] = (acc * per_row(1.0 / den)).astype(BF16)
        return carry

    lax.fori_loop(0, PER, one, 0)


def own_part(span, qkv):
    return pl.pallas_call(
        own_kernel,
        out_shape=(
            jax.ShapeDtypeStruct((PER, WIDTH, BLK), BF16),
            jax.ShapeDtypeStruct((PER, WIDTH, BLK), F32),
            jax.ShapeDtypeStruct((PER, 1, 2 * BLK), F32),
            jax.ShapeDtypeStruct((PER, 1, 2 * BLK), F32),
        ),
        in_specs=[SMEM, VMEM],
        out_specs=(VMEM,) * 4,
        scratch_shapes=[pltpu.VMEM((PER * BLK, WIDTH), BF16), pltpu.VMEM((PER * BLK, 2 * BLK), F32)],
        compiler_params=LIMIT,
        cost_estimate=cost(100_000_000_000),
        name="own_part",
    )(span, qkv)


def fold_rows(values, how):
    return how(values.reshape(BLK // 8, 8, 2 * BLK), axis=0)


def halo_kernel(side, pair_ref, kv_ref, q_ref, start_ref, acc_ref, max_ref, den_ref, out_ref, *scratch):
    keys, scores, tops, shifts, sums, dens = scratch
    pairs = pair_ref[side, 2 * SLOTS]
    steps = (pairs + STEP - 1) // STEP
    out_ref[...] = start_ref[...]

    @pl.when(pairs > 0)
    def _():
        for block in range(PER - 1):
            keys[block] = kv_ref[block, :WIDTH, :].T
        for block in range(PER):
            tops[block] = jnp.broadcast_to(max_ref[block], (8, 2 * BLK))

        def look(step, carry):
            for lane in range(STEP):
                pair = step * STEP + lane
                i, j = pair_ref[side, pair], pair_ref[side, SLOTS + pair]
                found = jnp.dot(keys[j], both_heads(q_ref[i, :WIDTH, :]), preferred_element_type=F32)
                scores[pair] = found
                tops[i] = jnp.maximum(tops[i], fold_rows(found, jnp.max))
            return carry

        lax.fori_loop(0, steps, look, 0)
        for block in range(PER):
            shifts[block] = jnp.max(tops[block], axis=0, keepdims=True) * SCALE_LOG2
        sums[...] = jnp.zeros_like(sums)
        dens[...] = jnp.zeros_like(dens)

        def weigh(step, carry):
            for lane in range(STEP):
                pair = step * STEP + lane
                i, j = pair_ref[side, pair], pair_ref[side, SLOTS + pair]
                shift = jnp.where(pair < pairs, shifts[i], FAR)
                weights = jnp.exp2(scores[pair] * SCALE_LOG2 - shift)
                dens[i] += fold_rows(weights, jnp.sum)
                sums[i] += diagonal(jnp.dot(kv_ref[j, WIDTH:, :], weights.astype(BF16), preferred_element_type=F32))
            return carry

        lax.fori_loop(0, steps, weigh, 0)

        def close(i, carry):
            fade = jnp.exp2(max_ref[i] * SCALE_LOG2 - shifts[i])
            share = 1.0 / (den_ref[i] * fade + jnp.sum(dens[i], axis=0, keepdims=True))
            out_ref[i] = (acc_ref[i] * per_row(fade * share) + sums[i] * per_row(share)).astype(BF16)
            return carry

        lax.fori_loop(pair_ref[side, 0], pair_ref[side, pairs - 1] + 1, close, 0)


def halo_part(side, pairs, kv, q, start, acc, top, den):
    return pl.pallas_call(
        functools.partial(halo_kernel, side),
        out_shape=jax.ShapeDtypeStruct((PER, WIDTH, BLK), BF16),
        in_specs=[SMEM] + [VMEM] * 6,
        out_specs=VMEM,
        scratch_shapes=[
            pltpu.VMEM((PER - 1, BLK, WIDTH), BF16),
            pltpu.VMEM((SLOTS, BLK, 2 * BLK), F32),
            pltpu.VMEM((PER, 8, 2 * BLK), F32),
            pltpu.VMEM((PER, 1, 2 * BLK), F32),
            pltpu.VMEM((PER, WIDTH, BLK), F32),
            pltpu.VMEM((PER, 8, 2 * BLK), F32),
        ],
        compiler_params=LIMIT,
        cost_estimate=cost(1_000_000_000),
        name="halo_part",
    )(pairs, kv, q, start, acc, top, den)


def shifted(value, steps):
    count = lax.axis_size("sup")
    pairs = [(i, i + steps) for i in range(count) if 0 <= i + steps < count]
    return lax.ppermute(value, "sup", pairs)


def spans(block_image):
    sup = lax.axis_index("sup")
    here = lax.dynamic_slice_in_dim(block_image, sup * PER, PER)
    low = jnp.sum((block_image[None, :] < here[:, None]).astype(jnp.int32), axis=1) - sup * PER
    high = jnp.sum((block_image[None, :] <= here[:, None]).astype(jnp.int32), axis=1) - sup * PER
    span = jnp.stack((jnp.maximum(low, 0), jnp.minimum(high, PER)))
    keys = jnp.stack((jnp.maximum(-jnp.min(low), 0), jnp.maximum(jnp.max(high) - PER, 0)))[:, None]
    queries = jnp.stack((jnp.sum((low < 0).astype(jnp.int32)), jnp.sum((high > PER).astype(jnp.int32))))[:, None]
    side = jnp.arange(2)[:, None]
    order = jnp.arange(SLOTS)[None, :]
    count = jnp.maximum(keys, 1)
    query = jnp.clip(jnp.where(side == 0, 0, PER - queries) + order // count, 0, PER - 1)
    key = jnp.where(side == 0, PER - 1 - count, 0) + order % count
    return span, jnp.concatenate((query, key, jnp.broadcast_to(keys * queries, (2, SLOTS))), axis=1)


def regrouped(parts):
    return lax.all_to_all(parts, ("core", "grp"), 0, 0, tiled=True)


def body(query_rows, key_rows, value_rows, block_image):
    span, pairs = spans(block_image)
    qkv = regrouped(split_heads(query_rows, key_rows, value_rows))
    rising = qkv[1:, WIDTH:]
    below = shifted(rising, 1)
    qkv, rising = lax.optimization_barrier((qkv, rising))
    above = shifted(qkv[:-1, WIDTH:], -1)
    start, acc, top, den = own_part(span, qkv)
    result = halo_part(1, pairs, above, qkv, start, acc, top, den)
    result = halo_part(0, pairs, below, qkv, result, acc, top, den)
    return join_heads(regrouped(result))


def solution(mesh):
    per_group = mesh.shape["grp"]
    cores = PER // per_group
    devices = mesh.devices.reshape(-1, cores, per_group)
    inner = jax.sharding.Mesh(devices, ("sup", "core", "grp"))
    rows = P(("sup", "core", "grp"), None)
    return jax.shard_map(
        body,
        mesh=inner,
        in_specs=(rows, rows, rows, P()),
        out_specs=rows,
        check_vma=False,
    )
```

time: 70.5 us -> 65.6 us (0.930)
  the two profiles are of different devices: /device:TPU:5 before, /device:TPU:6 now
where the time goes in v2:
time: 65.6 us; the launch traced here: 65 us
  starting transfers between devices  18.1 us (28%)
  Pallas kernels  15.7 us (24%)
  waiting for transfers between devices  14.5 us (22%)
  blocking collectives  10.4 us (16%)
  other arithmetic  4.28 us (7%)
  between operations  1.22 us (2%)
  local copies, waits for them, and re-layouts  0.9 us (1%)
    ppermute x2, starting transfers between devices, shifted(): return lax.ppermute(value, 'sup', pairs)  13.6 us
    all_to_all x1, blocking collectives, regrouped(): return lax.all_to_all(parts, ('core', 'grp'), 0, 0, tiled=True)  10.4 us
    all_to_all x1, waiting for transfers between devices, regrouped(): return lax.all_to_all(parts, ('core', 'grp'), 0, 0, tiled=True)  8.4 us
    pallas_call x1, Pallas kernels, own_part(): pl.pallas_call(own_kernel, out_shape=(jax.ShapeDtypeStruct((PER, WIDTH, B...  6.47 us
    ppermute x2, waiting for transfers between devices, shifted(): return lax.ppermute(value, 'sup', pairs)  6.06 us
    pallas_call x2, Pallas kernels, halo_part(): pl.pallas_call(functools.partial(halo_kernel, side), out_shape=jax.ShapeD...  6 us
    all_to_all x1, starting transfers between devices, regrouped(): return lax.all_to_all(parts, ('core', 'grp'), 0, 0, tiled=True)  4.48 us
    pallas_call x1, Pallas kernels, split_heads(): pl.pallas_call(split_kernel, out_shape=jax.ShapeDtypeStruct((PER, WIDTH *...  2.37 us
  transfers between devices with their start and end apart: 3, of which 2 were waited for; matrix products, arithmetic and copies ran while one was open for 7% of the time, Pallas kernels for 15%

profile of v2, /device:TPU:6, one launch (start us, length us, event | category | flops | bytes accessed | tf_op | source)
XLA Modules:
  0.0 65.0 jit_solution(12036661792731518456)
XLA Ops:
  0.0 2.4 %split_heads.1 = bf16[8,480,128]{2,1,0:T(8,128)(2,1)} custom-call(bf16[128,1280]{1,0:T(8,128)(2,1)} %refs_0_.1, bf16[128,1280]{1,0:T(8,128)(2,1)} %refs_1_.1, bf16[128,1280]{1,0:T(8,128)(2,1)} %refs_2_.1), custom_call_target="tpu_custom_call" | custom-call | flops 1500000000 | bytes 1000000 | tf_op jit(solution)/shard_map/split_heads/pallas_call | solution.py:54
  2.4 4.5 %all-to-all-start = ((bf16[8,480,128]{2,1,0:T(8,128)(2,1)}), bf16[8,480,128]{2,1,0:T(8,128)(2,1)S(1)}, u32[]{:S(2)}, u32[]{:S(2)}) async-start(bf16[8,480,128]{2,1,0:T(8,128)(2,1)} %split_heads.1), calls=%async_computation | async-start | bytes 1966080 | tf_op jit(solution)/shard_map/all_to_all | solution.py:248
  6.9 0.0 copy-start
  6.9 0.7 %copy-done = s32[512]{0:T(512)S(1)} copy-done((s32[512]{0:T(512)S(1)}, s32[512]{0:T(512)}, u32[]{:S(2)}) %copy-start) | copy-done | bytes 2072
  7.6 0.1 dynamic_slice.3
  7.6 0.2 convert_reduce_fusion.1
  7.8 0.7 %fusion.1 = (s32[]{:T(128)}, s32[]{:T(128)}, s32[1,8]{1,0:T(1,128)S(1)}, s32[1,8]{1,0:T(1,128)S(1)}, s32[]{:T(128)}, /*index=5*/s32[]{:T(128)}) fusion(s32[8]{0:T(128)S(1)} %get-tuple-element.15, s32[]{:T(128)S(6)} %mul.13, s32[8]{0:T(128)S(1)} %get-tuple-element.16), kind=kLoop, calls=%fused_computation.13 | loop fusion | flops 92 | bytes 148 | tf_op jit(solution)/shard_map/reduce_sum | solution.py:238
  9.7 0.1 fusion.6
  9.8 1.4 %fusion.3 = s32[2]{0:T(128)S(1)} fusion(s32[1]{0:T(128)} %bitcast.3, s32[1]{0:T(128)} %bitcast.2, s32[1]{0:T(128)} %bitcast.1, s32[1]{0:T(128)} %bitcast), kind=kLoop, calls=%fused_computation.23 | loop fusion | flops 6 | bytes 24 | tf_op jit(solution)/shard_map/mul | solution.py:244
  11.2 1.4 %compare_select_fusion.2 = s32[2]{0:T(128)S(1)} fusion(s32[1]{0:T(128)} %bitcast.1, s32[1]{0:T(128)} %bitcast), kind=kLoop, calls=%fused_computation.8 | loop fusion | flops 8 | bytes 16 | tf_op jit(solution)/shard_map/jit(_where)/select_n | solution.py:242
  12.6 0.2 fusion
  12.8 0.2 add_clamp_fusion
  13.0 0.1 broadcast_in_dim.4
  13.0 0.1 pad_add_fusion.pair_ref
  13.1 8.4 %all-to-all-done.qkv_ref.q_ref = bf16[8,480,128]{2,1,0:T(8,128)(2,1)S(1)} async-done(((bf16[8,480,128]{2,1,0:T(8,128)(2,1)}), bf16[8,480,128]{2,1,0:T(8,128)(2,1)S(1)}, u32[]{:S(2)}, u32[]{:S(2)}) %all-to-all-start) | async-done | bytes 983072 | tf_op jit(solution)/shard_map/all_to_all | solution.py:248
  21.5 3.8 %collective-permute-start = (bf16[7,320,128]{2,1,0:T(8,128)(2,1)S(1)}, bf16[7,320,128]{2,1,0:T(8,128)(2,1)S(1)}, u32[]{:S(2)}, u32[]{:S(2)}) collective-permute-start(bf16[7,320,128]{2,1,0:T(8,128)(2,1)S(1)} %slice.8), channel_id=1, source_target_pairs={{0,8},{8,16},{16,24},{24,32},{32,40},{40,48},{48,56},{56,64},{64,7... | collective-permute-start | bytes 1720328 | tf_op jit(solution)/shard_map/ppermute | solution.py:228
  25.4 9.8 %collective-permute-start.1 = (bf16[7,320,128]{2,1,0:T(8,128)(2,1)S(1)}, bf16[7,320,128]{2,1,0:T(8,128)(2,1)S(1)}, u32[]{:S(2)}, u32[]{:S(2)}) collective-permute-start(bf16[7,320,128]{2,1,0:T(8,128)(2,1)S(1)} %slice.7), channel_id=1, source_target_pairs={{8,0},{16,8},{24,16},{32,24},{40,32},{48,40},{56,48},{64,56},{72,6... | collective-permute-start | bytes 1720328 | tf_op jit(solution)/shard_map/ppermute | solution.py:228
  35.2 6.5 %own_part.1 = (bf16[8,160,128]{2,1,0:T(8,128)(2,1)S(1)}, f32[8,160,128]{2,1,0:T(8,128)S(1)}, f32[8,1,256]{2,1,0:T(1,128)S(1)}, f32[8,1,256]{2,1,0:T(1,128)S(1)}) custom-call(s32[2,8]{1,0:T(2,128)S(1)} %pad_add_fusion.1.span_ref, bf16[8,480,128]{2,1,0:T(8,128)(2,1)S(1)} %all-to-all-done.qkv_ref.q_ref), custom_call_target="tpu_custom_call" | custom-call | flops 99999997952 | bytes 1000000 | tf_op jit(solution)/shard_map/own_part/pallas_call | solution.py:135
  41.7 6.1 %collective-permute-done.1.kv_ref = bf16[7,320,128]{2,1,0:T(8,128)(2,1)S(1)} collective-permute-done((bf16[7,320,128]{2,1,0:T(8,128)(2,1)S(1)}, bf16[7,320,128]{2,1,0:T(8,128)(2,1)S(1)}, u32[]{:S(2)}, u32[]{:S(2)}) %collective-permute-start.1) | collective-permute-done | bytes 573472 | tf_op jit(solution)/shard_map/ppermute | solution.py:228
  47.7 3.0 %halo_part.2.start_ref = bf16[8,160,128]{2,1,0:T(8,128)(2,1)S(1)} custom-call(s32[2,48]{1,0:T(2,128)S(1)} %pad_add_fusion.pair_ref, bf16[7,320,128]{2,1,0:T(8,128)(2,1)S(1)} %collective-permute-done.1.kv_ref, bf16[8,480,128]{2,1,0:T(8,128)(2,1)S(1)} %all-to-all-done.qkv_ref.q_ref, bf16[8,160,128]{2,1,0:T(8,128)(2,1)S(1)} %get-tuple-element.11.start_ref, ...), custom_call_target="tpu_custom_call" | custom-call | flops 1000000000 | bytes 1000000 | tf_op jit(solution)/shard_map/halo_part/pallas_call | solution.py:206
  50.7 0.0 collective-permute-done.kv_ref
  50.7 3.0 %halo_part.3 = bf16[8,160,128]{2,1,0:T(8,128)(2,1)S(1)} custom-call(s32[2,48]{1,0:T(2,128)S(1)} %pad_add_fusion.pair_ref, bf16[7,320,128]{2,1,0:T(8,128)(2,1)S(1)} %collective-permute-done.kv_ref, bf16[8,480,128]{2,1,0:T(8,128)(2,1)S(1)} %all-to-all-done.qkv_ref.q_ref, bf16[8,160,128]{2,1,0:T(8,128)(2,1)S(1)} %halo_part.2.start_ref, ...), custom_call_target="tpu_custom_call" | custom-call | flops 1000000000 | bytes 1000000 | tf_op jit(solution)/shard_map/halo_part/pallas_call | solution.py:206
  53.7 10.4 %all_to_all.10.in_ref = bf16[8,160,128]{2,1,0:T(8,128)(2,1)S(1)} all-to-all(bf16[8,160,128]{2,1,0:T(8,128)(2,1)S(1)} %halo_part.3), channel_id=1, replica_groups=mesh['sup'=64,'core'=2,'grp'=4] {'core','grp'}, dimensions={0} | all-to-all | bytes 655360 | tf_op jit(solution)/shard_map/all_to_all | solution.py:248
  64.1 0.9 %join_heads.1 = bf16[128,1280]{1,0:T(8,128)(2,1)} custom-call(bf16[8,160,128]{2,1,0:T(8,128)(2,1)S(1)} %all_to_all.10.in_ref), custom_call_target="tpu_custom_call" | custom-call | tf_op jit(solution)/shard_map/join_heads/pallas_call | solution.py:70
  (5 shorter events, 0.1 us)
Async XLA Ops:
  2.4 19.1 %all-to-all-start = ((bf16[8,480,128]{2,1,0:T(8,128)(2,1)}), bf16[8,480,128]{2,1,0:T(8,128)(2,1)S(1)}, u32[]{:S(2)}, u32[]{:S(2)}) async-start(bf16[8,480,128]{2,1,0:T(8,128)(2,1)} %split_heads.1), calls=%async_computation | async-start | bytes 1966080 | tf_op jit(solution)/shard_map/all_to_all | solution.py:248
  6.9 0.7 %copy-start = (s32[512]{0:T(512)S(1)}, s32[512]{0:T(512)}, u32[]{:S(2)}) copy-start(s32[512]{0:T(512)} %param.7) | copy-start | bytes 6148
  21.5 29.2 %collective-permute-start = (bf16[7,320,128]{2,1,0:T(8,128)(2,1)S(1)}, bf16[7,320,128]{2,1,0:T(8,128)(2,1)S(1)}, u32[]{:S(2)}, u32[]{:S(2)}) collective-permute-start(bf16[7,320,128]{2,1,0:T(8,128)(2,1)S(1)} %slice.8), channel_id=1, source_target_pairs={{0,8},{8,16},{16,24},{24,32},{32,40},{40,48},{48,56},{56,64},{64,7... | collective-permute-start | bytes 1720328 | tf_op jit(solution)/shard_map/ppermute | solution.py:228
  25.4 22.3 %collective-permute-start.1 = (bf16[7,320,128]{2,1,0:T(8,128)(2,1)S(1)}, bf16[7,320,128]{2,1,0:T(8,128)(2,1)S(1)}, u32[]{:S(2)}, u32[]{:S(2)}) collective-permute-start(bf16[7,320,128]{2,1,0:T(8,128)(2,1)S(1)} %slice.7), channel_id=1, source_target_pairs={{8,0},{16,8},{24,16},{32,24},{40,32},{48,40},{56,48},{64,56},{72,6... | collective-permute-start | bytes 1720328 | tf_op jit(solution)/shard_map/ppermute | solution.py:228

commit v3 on v2

--- a/solution.py
+++ b/solution.py
@@ -256,8 +256,8 @@
     qkv, rising = lax.optimization_barrier((qkv, rising))
     above = shifted(qkv[:-1, WIDTH:], -1)
     start, acc, top, den = own_part(span, qkv)
-    result = halo_part(1, pairs, above, qkv, start, acc, top, den)
-    result = halo_part(0, pairs, below, qkv, result, acc, top, den)
+    result = halo_part(0, pairs, below, qkv, start, acc, top, den)
+    result = halo_part(1, pairs, above, qkv, result, acc, top, den)
     return join_heads(regrouped(result))
 
 

time: 65.6 us -> 63.3 us (0.965)
  waiting for transfers between devices: 14.5 us -> 13.2 us
  Pallas kernels: 15.7 us -> 14.7 us
    ppermute x2, waiting for transfers between devices: 6.06 us -> 4.83 us  [shifted(): return lax.ppermute(value, 'sup', pairs)]
    pallas_call x2, Pallas kernels: 6 us -> 4.96 us  [halo_part(): pl.pallas_call(functools.partial(halo_kernel, side), out_shape=jax.ShapeD...]
  transfers between devices with their start and end apart: 3 -> 3, of which waited for: 2 -> 2; matrix products, arithmetic and copies ran while one was open for 7% -> 7% of each run, Pallas kernels for 15% -> 13%
where the time goes in v3:
time: 63.3 us; the launch traced here: 62.7 us
  starting transfers between devices  18.1 us (29%)
  Pallas kernels  14.7 us (23%)
  waiting for transfers between devices  13.2 us (21%)
  blocking collectives  10.4 us (16%)
  other arithmetic  4.28 us (7%)
  between operations  1.21 us (2%)
  local copies, waits for them, and re-layouts  0.9 us (1%)
    ppermute x2, starting transfers between devices, shifted(): return lax.ppermute(value, 'sup', pairs)  13.6 us
    all_to_all x1, blocking collectives, regrouped(): return lax.all_to_all(parts, ('core', 'grp'), 0, 0, tiled=True)  10.4 us
    all_to_all x1, waiting for transfers between devices, regrouped(): return lax.all_to_all(parts, ('core', 'grp'), 0, 0, tiled=True)  8.4 us
    pallas_call x1, Pallas kernels, own_part(): pl.pallas_call(own_kernel, out_shape=(jax.ShapeDtypeStruct((PER, WIDTH, B...  6.47 us
    pallas_call x2, Pallas kernels, halo_part(): pl.pallas_call(functools.partial(halo_kernel, side), out_shape=jax.ShapeD...  4.96 us
    ppermute x2, waiting for transfers between devices, shifted(): return lax.ppermute(value, 'sup', pairs)  4.83 us
    all_to_all x1, starting transfers between devices, regrouped(): return lax.all_to_all(parts, ('core', 'grp'), 0, 0, tiled=True)  4.48 us
    pallas_call x1, Pallas kernels, split_heads(): pl.pallas_call(split_kernel, out_shape=jax.ShapeDtypeStruct((PER, WIDTH *...  2.37 us
  transfers between devices with their start and end apart: 3, of which 2 were waited for; matrix products, arithmetic and copies ran while one was open for 7% of the time, Pallas kernels for 13%

profile of v3, /device:TPU:6, one launch (start us, length us, event | category | flops | bytes accessed | tf_op | source)
XLA Modules:
  0.0 62.7 jit_solution(7032257825752876794)
XLA Ops:
  0.0 2.4 %split_heads.1 = bf16[8,480,128]{2,1,0:T(8,128)(2,1)} custom-call(bf16[128,1280]{1,0:T(8,128)(2,1)} %refs_0_.1, bf16[128,1280]{1,0:T(8,128)(2,1)} %refs_1_.1, bf16[128,1280]{1,0:T(8,128)(2,1)} %refs_2_.1), custom_call_target="tpu_custom_call" | custom-call | flops 1500000000 | bytes 1000000 | tf_op jit(solution)/shard_map/split_heads/pallas_call | solution.py:54
  2.4 4.5 %all-to-all-start = ((bf16[8,480,128]{2,1,0:T(8,128)(2,1)}), bf16[8,480,128]{2,1,0:T(8,128)(2,1)S(1)}, u32[]{:S(2)}, u32[]{:S(2)}) async-start(bf16[8,480,128]{2,1,0:T(8,128)(2,1)} %split_heads.1), calls=%async_computation | async-start | bytes 1966080 | tf_op jit(solution)/shard_map/all_to_all | solution.py:248
  6.9 0.0 copy-start
  6.9 0.7 %copy-done = s32[512]{0:T(512)S(1)} copy-done((s32[512]{0:T(512)S(1)}, s32[512]{0:T(512)}, u32[]{:S(2)}) %copy-start) | copy-done | bytes 2072
  7.6 0.1 dynamic_slice.3
  7.6 0.2 convert_reduce_fusion.1
  7.8 0.7 %fusion.1 = (s32[]{:T(128)}, s32[]{:T(128)}, s32[1,8]{1,0:T(1,128)S(1)}, s32[1,8]{1,0:T(1,128)S(1)}, s32[]{:T(128)}, /*index=5*/s32[]{:T(128)}) fusion(s32[8]{0:T(128)S(1)} %get-tuple-element.15, s32[]{:T(128)S(6)} %mul.13, s32[8]{0:T(128)S(1)} %get-tuple-element.16), kind=kLoop, calls=%fused_computation.13 | loop fusion | flops 92 | bytes 148 | tf_op jit(solution)/shard_map/reduce_sum | solution.py:238
  9.7 0.1 fusion.6
  9.8 1.4 %compare_select_fusion.2 = s32[2]{0:T(128)S(1)} fusion(s32[1]{0:T(128)} %bitcast.1, s32[1]{0:T(128)} %bitcast), kind=kLoop, calls=%fused_computation.8 | loop fusion | flops 8 | bytes 16 | tf_op jit(solution)/shard_map/jit(_where)/select_n | solution.py:242
  11.2 1.4 %fusion.3 = s32[2]{0:T(128)S(1)} fusion(s32[1]{0:T(128)} %bitcast.3, s32[1]{0:T(128)} %bitcast.2, s32[1]{0:T(128)} %bitcast.1, s32[1]{0:T(128)} %bitcast), kind=kLoop, calls=%fused_computation.23 | loop fusion | flops 6 | bytes 24 | tf_op jit(solution)/shard_map/mul | solution.py:244
  12.6 0.2 fusion
  12.8 0.2 add_clamp_fusion
  13.0 0.1 broadcast_in_dim.4
  13.0 0.1 pad_add_fusion.pair_ref
  13.1 8.4 %all-to-all-done.qkv_ref.q_ref = bf16[8,480,128]{2,1,0:T(8,128)(2,1)S(1)} async-done(((bf16[8,480,128]{2,1,0:T(8,128)(2,1)}), bf16[8,480,128]{2,1,0:T(8,128)(2,1)S(1)}, u32[]{:S(2)}, u32[]{:S(2)}) %all-to-all-start) | async-done | bytes 983072 | tf_op jit(solution)/shard_map/all_to_all | solution.py:248
  21.5 3.8 %collective-permute-start.1 = (bf16[7,320,128]{2,1,0:T(8,128)(2,1)S(1)}, bf16[7,320,128]{2,1,0:T(8,128)(2,1)S(1)}, u32[]{:S(2)}, u32[]{:S(2)}) collective-permute-start(bf16[7,320,128]{2,1,0:T(8,128)(2,1)S(1)} %slice.8), channel_id=1, source_target_pairs={{0,8},{8,16},{16,24},{24,32},{32,40},{40,48},{48,56},{56,64},{64,7... | collective-permute-start | bytes 1720328 | tf_op jit(solution)/shard_map/ppermute | solution.py:228
  25.4 9.8 %collective-permute-start = (bf16[7,320,128]{2,1,0:T(8,128)(2,1)S(1)}, bf16[7,320,128]{2,1,0:T(8,128)(2,1)S(1)}, u32[]{:S(2)}, u32[]{:S(2)}) collective-permute-start(bf16[7,320,128]{2,1,0:T(8,128)(2,1)S(1)} %slice.7), channel_id=1, source_target_pairs={{8,0},{16,8},{24,16},{32,24},{40,32},{48,40},{56,48},{64,56},{72,6... | collective-permute-start | bytes 1720328 | tf_op jit(solution)/shard_map/ppermute | solution.py:228
  35.2 6.5 %own_part.1 = (bf16[8,160,128]{2,1,0:T(8,128)(2,1)S(1)}, f32[8,160,128]{2,1,0:T(8,128)S(1)}, f32[8,1,256]{2,1,0:T(1,128)S(1)}, f32[8,1,256]{2,1,0:T(1,128)S(1)}) custom-call(s32[2,8]{1,0:T(2,128)S(1)} %pad_add_fusion.1.span_ref, bf16[8,480,128]{2,1,0:T(8,128)(2,1)S(1)} %all-to-all-done.qkv_ref.q_ref), custom_call_target="tpu_custom_call" | custom-call | flops 99999997952 | bytes 1000000 | tf_op jit(solution)/shard_map/own_part/pallas_call | solution.py:135
  41.7 4.8 %collective-permute-done.1.kv_ref = bf16[7,320,128]{2,1,0:T(8,128)(2,1)S(1)} collective-permute-done((bf16[7,320,128]{2,1,0:T(8,128)(2,1)S(1)}, bf16[7,320,128]{2,1,0:T(8,128)(2,1)S(1)}, u32[]{:S(2)}, u32[]{:S(2)}) %collective-permute-start.1) | collective-permute-done | bytes 573472 | tf_op jit(solution)/shard_map/ppermute | solution.py:228
  46.5 1.9 %halo_part.2.start_ref = bf16[8,160,128]{2,1,0:T(8,128)(2,1)S(1)} custom-call(s32[2,48]{1,0:T(2,128)S(1)} %pad_add_fusion.pair_ref, bf16[7,320,128]{2,1,0:T(8,128)(2,1)S(1)} %collective-permute-done.1.kv_ref, bf16[8,480,128]{2,1,0:T(8,128)(2,1)S(1)} %all-to-all-done.qkv_ref.q_ref, bf16[8,160,128]{2,1,0:T(8,128)(2,1)S(1)} %get-tuple-element.11.start_ref, ...), custom_call_target="tpu_custom_call" | custom-call | flops 1000000000 | bytes 1000000 | tf_op jit(solution)/shard_map/halo_part/pallas_call | solution.py:206
  48.4 0.0 collective-permute-done.kv_ref
  48.4 3.0 %halo_part.3 = bf16[8,160,128]{2,1,0:T(8,128)(2,1)S(1)} custom-call(s32[2,48]{1,0:T(2,128)S(1)} %pad_add_fusion.pair_ref, bf16[7,320,128]{2,1,0:T(8,128)(2,1)S(1)} %collective-permute-done.kv_ref, bf16[8,480,128]{2,1,0:T(8,128)(2,1)S(1)} %all-to-all-done.qkv_ref.q_ref, bf16[8,160,128]{2,1,0:T(8,128)(2,1)S(1)} %halo_part.2.start_ref, ...), custom_call_target="tpu_custom_call" | custom-call | flops 1000000000 | bytes 1000000 | tf_op jit(solution)/shard_map/halo_part/pallas_call | solution.py:206
  51.5 10.4 %all_to_all.10.in_ref = bf16[8,160,128]{2,1,0:T(8,128)(2,1)S(1)} all-to-all(bf16[8,160,128]{2,1,0:T(8,128)(2,1)S(1)} %halo_part.3), channel_id=1, replica_groups=mesh['sup'=64,'core'=2,'grp'=4] {'core','grp'}, dimensions={0} | all-to-all | bytes 655360 | tf_op jit(solution)/shard_map/all_to_all | solution.py:248
  61.8 0.9 %join_heads.1 = bf16[128,1280]{1,0:T(8,128)(2,1)} custom-call(bf16[8,160,128]{2,1,0:T(8,128)(2,1)S(1)} %all_to_all.10.in_ref), custom_call_target="tpu_custom_call" | custom-call | tf_op jit(solution)/shard_map/join_heads/pallas_call | solution.py:70
  (5 shorter events, 0.1 us)
Async XLA Ops:
  2.4 19.1 %all-to-all-start = ((bf16[8,480,128]{2,1,0:T(8,128)(2,1)}), bf16[8,480,128]{2,1,0:T(8,128)(2,1)S(1)}, u32[]{:S(2)}, u32[]{:S(2)}) async-start(bf16[8,480,128]{2,1,0:T(8,128)(2,1)} %split_heads.1), calls=%async_computation | async-start | bytes 1966080 | tf_op jit(solution)/shard_map/all_to_all | solution.py:248
  6.9 0.7 %copy-start = (s32[512]{0:T(512)S(1)}, s32[512]{0:T(512)}, u32[]{:S(2)}) copy-start(s32[512]{0:T(512)} %param.7) | copy-start | bytes 6148
  21.5 25.0 %collective-permute-start.1 = (bf16[7,320,128]{2,1,0:T(8,128)(2,1)S(1)}, bf16[7,320,128]{2,1,0:T(8,128)(2,1)S(1)}, u32[]{:S(2)}, u32[]{:S(2)}) collective-permute-start(bf16[7,320,128]{2,1,0:T(8,128)(2,1)S(1)} %slice.8), channel_id=1, source_target_pairs={{0,8},{8,16},{16,24},{24,32},{32,40},{40,48},{48,56},{56,64},{64,7... | collective-permute-start | bytes 1720328 | tf_op jit(solution)/shard_map/ppermute | solution.py:228
  25.4 23.0 %collective-permute-start = (bf16[7,320,128]{2,1,0:T(8,128)(2,1)S(1)}, bf16[7,320,128]{2,1,0:T(8,128)(2,1)S(1)}, u32[]{:S(2)}, u32[]{:S(2)}) collective-permute-start(bf16[7,320,128]{2,1,0:T(8,128)(2,1)S(1)} %slice.7), channel_id=1, source_target_pairs={{8,0},{16,8},{24,16},{32,24},{40,32},{48,40},{56,48},{64,56},{72,6... | collective-permute-start | bytes 1720328 | tf_op jit(solution)/shard_map/ppermute | solution.py:228

commit v4 on v3

--- a/solution.py
+++ b/solution.py
@@ -17,7 +17,7 @@
 SCALE_LOG2 = math.log2(math.e) / math.sqrt(HDIM)
 FAR = 1e30
 SLOTS = 16
-STEP = 4
+STEP = 8
 VMEM = pl.BlockSpec(memory_space=pltpu.VMEM)
 SMEM = pl.BlockSpec(memory_space=pltpu.SMEM)
 HBM = pl.BlockSpec(memory_space=pltpu.HBM)
@@ -97,12 +97,16 @@
     )
 
 
-def own_kernel(span_ref, qkv_ref, out_ref, acc_ref, max_ref, den_ref, keys, scores):
+def own_kernel(image_ref, qkv_ref, out_ref, acc_ref, max_ref, den_ref, keys, scores):
     for block in range(PER):
         keys[block * BLK : (block + 1) * BLK, :] = qkv_ref[block, WIDTH : 2 * WIDTH, :].T
 
+    group = lax.axis_index("sup") * PER
+
     def one(i, carry):
-        first, last = span_ref[0, i], span_ref[1, i]
+        image = image_ref[group + i]
+        first = sum((image_ref[group + j] < image).astype(jnp.int32) for j in range(PER))
+        last = sum((image_ref[group + j] <= image).astype(jnp.int32) for j in range(PER))
         weights_in = both_heads(qkv_ref[i, :WIDTH, :])
         top = jnp.full((1, 2 * BLK), -FAR, F32)
         for j in range(PER):
@@ -131,7 +135,7 @@
     lax.fori_loop(0, PER, one, 0)
 
 
-def own_part(span, qkv):
+def own_part(image, qkv):
     return pl.pallas_call(
         own_kernel,
         out_shape=(
@@ -146,17 +150,35 @@
         compiler_params=LIMIT,
         cost_estimate=cost(100_000_000_000),
         name="own_part",
-    )(span, qkv)
+    )(image, qkv)
 
 
 def fold_rows(values, how):
     return how(values.reshape(BLK // 8, 8, 2 * BLK), axis=0)
 
 
-def halo_kernel(side, pair_ref, kv_ref, q_ref, start_ref, acc_ref, max_ref, den_ref, out_ref, *scratch):
+def halo_kernel(side, image_ref, kv_ref, q_ref, start_ref, acc_ref, max_ref, den_ref, out_ref, *scratch):
     keys, scores, tops, shifts, sums, dens = scratch
-    pairs = pair_ref[side, 2 * SLOTS]
+    place, places = lax.axis_index("sup"), lax.axis_size("sup")
+    group = place * PER
+    if side == 0:
+        image, beyond = image_ref[group], jnp.maximum(group - (PER - 1), 0)
+        there = place > 0
+    else:
+        image, beyond = image_ref[group + PER - 1], jnp.minimum(group + PER, (places - 1) * PER)
+        there = place < places - 1
+    count = sum((there & (image_ref[beyond + j] == image)).astype(jnp.int32) for j in range(PER - 1))
+    queries = sum((image_ref[group + j] == image).astype(jnp.int32) for j in range(PER))
+    pairs = count * queries
+    first_query = 0 if side == 0 else PER - queries
+    first_key = PER - 1 - count if side == 0 else 0
     steps = (pairs + STEP - 1) // STEP
+
+    def advance(at):
+        i, j = at
+        wrap = j + 1 == count
+        return jnp.where(wrap, jnp.minimum(i + 1, PER - 1), i), jnp.where(wrap, 0, j + 1)
+
     out_ref[...] = start_ref[...]
 
     @pl.when(pairs > 0)
@@ -166,32 +188,35 @@
         for block in range(PER):
             tops[block] = jnp.broadcast_to(max_ref[block], (8, 2 * BLK))
 
-        def look(step, carry):
+        def look(step, at):
             for lane in range(STEP):
                 pair = step * STEP + lane
-                i, j = pair_ref[side, pair], pair_ref[side, SLOTS + pair]
+                i, j = at[0], first_key + at[1]
+                at = advance(at)
                 found = jnp.dot(keys[j], both_heads(q_ref[i, :WIDTH, :]), preferred_element_type=F32)
                 scores[pair] = found
                 tops[i] = jnp.maximum(tops[i], fold_rows(found, jnp.max))
-            return carry
-
-        lax.fori_loop(0, steps, look, 0)
+            return at
+
+        start = (jnp.int32(first_query), jnp.int32(0))
+        lax.fori_loop(0, steps, look, start)
         for block in range(PER):
             shifts[block] = jnp.max(tops[block], axis=0, keepdims=True) * SCALE_LOG2
         sums[...] = jnp.zeros_like(sums)
         dens[...] = jnp.zeros_like(dens)
 
-        def weigh(step, carry):
+        def weigh(step, at):
             for lane in range(STEP):
                 pair = step * STEP + lane
-                i, j = pair_ref[side, pair], pair_ref[side, SLOTS + pair]
+                i, j = at[0], first_key + at[1]
+                at = advance(at)
                 shift = jnp.where(pair < pairs, shifts[i], FAR)
                 weights = jnp.exp2(scores[pair] * SCALE_LOG2 - shift)
                 dens[i] += fold_rows(weights, jnp.sum)
                 sums[i] += diagonal(jnp.dot(kv_ref[j, WIDTH:, :], weights.astype(BF16), preferred_element_type=F32))
-            return carry
-
-        lax.fori_loop(0, steps, weigh, 0)
+            return at
+
+        lax.fori_loop(0, steps, weigh, start)
 
         def close(i, carry):
             fade = jnp.exp2(max_ref[i] * SCALE_LOG2 - shifts[i])
@@ -199,10 +224,10 @@
             out_ref[i] = (acc_ref[i] * per_row(fade * share) + sums[i] * per_row(share)).astype(BF16)
             return carry
 
-        lax.fori_loop(pair_ref[side, 0], pair_ref[side, pairs - 1] + 1, close, 0)
-
-
-def halo_part(side, pairs, kv, q, start, acc, top, den):
+        lax.fori_loop(first_query, first_query + queries, close, 0)
+
+
+def halo_part(side, image, kv, q, start, acc, top, den):
     return pl.pallas_call(
         functools.partial(halo_kernel, side),
         out_shape=jax.ShapeDtypeStruct((PER, WIDTH, BLK), BF16),
@@ -219,7 +244,7 @@
         compiler_params=LIMIT,
         cost_estimate=cost(1_000_000_000),
         name="halo_part",
-    )(pairs, kv, q, start, acc, top, den)
+    )(image, kv, q, start, acc, top, den)
 
 
 def shifted(value, steps):
@@ -228,36 +253,19 @@
     return lax.ppermute(value, "sup", pairs)
 
 
-def spans(block_image):
-    sup = lax.axis_index("sup")
-    here = lax.dynamic_slice_in_dim(block_image, sup * PER, PER)
-    low = jnp.sum((block_image[None, :] < here[:, None]).astype(jnp.int32), axis=1) - sup * PER
-    high = jnp.sum((block_image[None, :] <= here[:, None]).astype(jnp.int32), axis=1) - sup * PER
-    span = jnp.stack((jnp.maximum(low, 0), jnp.minimum(high, PER)))
-    keys = jnp.stack((jnp.maximum(-jnp.min(low), 0), jnp.maximum(jnp.max(high) - PER, 0)))[:, None]
-    queries = jnp.stack((jnp.sum((low < 0).astype(jnp.int32)), jnp.sum((high > PER).astype(jnp.int32))))[:, None]
-    side = jnp.arange(2)[:, None]
-    order = jnp.arange(SLOTS)[None, :]
-    count = jnp.maximum(keys, 1)
-    query = jnp.clip(jnp.where(side == 0, 0, PER - queries) + order // count, 0, PER - 1)
-    key = jnp.where(side == 0, PER - 1 - count, 0) + order % count
-    return span, jnp.concatenate((query, key, jnp.broadcast_to(keys * queries, (2, SLOTS))), axis=1)
-
-
 def regrouped(parts):
     return lax.all_to_all(parts, ("core", "grp"), 0, 0, tiled=True)
 
 
 def body(query_rows, key_rows, value_rows, block_image):
-    span, pairs = spans(block_image)
     qkv = regrouped(split_heads(query_rows, key_rows, value_rows))
     rising = qkv[1:, WIDTH:]
     below = shifted(rising, 1)
     qkv, rising = lax.optimization_barrier((qkv, rising))
     above = shifted(qkv[:-1, WIDTH:], -1)
-    start, acc, top, den = own_part(span, qkv)
-    result = halo_part(0, pairs, below, qkv, start, acc, top, den)
-    result = halo_part(1, pairs, above, qkv, result, acc, top, den)
+    start, acc, top, den = own_part(block_image, qkv)
+    result = halo_part(0, block_image, below, qkv, start, acc, top, den)
+    result = halo_part(1, block_image, above, qkv, result, acc, top, den)
     return join_heads(regrouped(result))
 
 

time: 63.3 us -> 61.3 us (0.968)
  blocking collectives: 10.4 us -> 29.5 us
  waiting for transfers between devices: 13.2 us -> 5.3 us
  starting transfers between devices: 18.1 us -> 13.6 us
  other arithmetic: 4.28 us -> 0 us
  Pallas kernels: 14.7 us -> 12 us
  between operations: 1.21 us -> 0.08 us
  local copies, waits for them, and re-layouts: 0.9 us -> 0.08 us
    all_to_all x1 -> x2, blocking collectives: 10.4 us -> 29.5 us  [regrouped(): return lax.all_to_all(parts, ('core', 'grp'), 0, 0, tiled=True)]
    all_to_all x1 -> x0, waiting for transfers between devices: 8.4 us -> none  [regrouped(): return lax.all_to_all(parts, ('core', 'grp'), 0, 0, tiled=True)]
    all_to_all x1 -> x0, starting transfers between devices: 4.48 us -> none  [regrouped(): return lax.all_to_all(parts, ('core', 'grp'), 0, 0, tiled=True)]
    pallas_call x2, Pallas kernels: 4.96 us -> 2.16 us  [halo_part(): pl.pallas_call(functools.partial(halo_kernel, side), out_shape=jax.ShapeD...]
    select_n x2 -> x0, other arithmetic: 1.4 us -> none  [the longest x1 1.39 us: spans(): jnp.where(side == 0, 0, PER - queries) + order // count]
    mul x1 -> x0, other arithmetic: 1.4 us -> none  [spans(): keys * queries]
    reduce_sum x2 -> x0, other arithmetic: 0.93 us -> none  [the longest x1 0.74 us: spans(): jnp.sum((low < 0).astype(jnp.int32))]
    unnamed x2, local copies, waits for them, and re-layouts: 0.68 us -> 0.01 us
  transfers between devices with their start and end apart: 3 -> 2, of which waited for: 2 -> 2; matrix products, arithmetic and copies ran while one was open for 7% -> 0% of each run, Pallas kernels for 13% -> 12%
where the time goes in v4:
time: 61.3 us; the launch traced here: 60.6 us
  blocking collectives  29.5 us (48%)
  starting transfers between devices  13.6 us (22%)
  Pallas kernels  12 us (20%)
  waiting for transfers between devices  5.3 us (9%)
    all_to_all x2, blocking collectives, regrouped(): return lax.all_to_all(parts, ('core', 'grp'), 0, 0, tiled=True)  29.5 us
    ppermute x2, starting transfers between devices, shifted(): return lax.ppermute(value, 'sup', pairs)  13.6 us
    pallas_call x1, Pallas kernels, own_part(): pl.pallas_call(own_kernel, out_shape=(jax.ShapeDtypeStruct((PER, WIDTH, B...  6.56 us
    ppermute x2, waiting for transfers between devices, shifted(): return lax.ppermute(value, 'sup', pairs)  5.3 us
    pallas_call x1, Pallas kernels, split_heads(): pl.pallas_call(split_kernel, out_shape=jax.ShapeDtypeStruct((PER, WIDTH *...  2.38 us
    pallas_call x2, Pallas kernels, halo_part(): pl.pallas_call(functools.partial(halo_kernel, side), out_shape=jax.ShapeD...  2.16 us
  transfers between devices with their start and end apart: 2, of which 2 were waited for; matrix products, arithmetic and copies ran while one was open for 0% of the time, Pallas kernels for 12%

profile of v4, /device:TPU:6, one launch (start us, length us, event | category | flops | bytes accessed | tf_op | source)
XLA Modules:
  0.0 60.6 jit_solution(11590741748449665208)
XLA Ops:
  0.0 2.4 %split_heads.1 = bf16[8,480,128]{2,1,0:T(8,128)(2,1)} custom-call(bf16[128,1280]{1,0:T(8,128)(2,1)} %refs_0_.1, bf16[128,1280]{1,0:T(8,128)(2,1)} %refs_1_.1, bf16[128,1280]{1,0:T(8,128)(2,1)} %refs_2_.1), custom_call_target="tpu_custom_call" | custom-call | flops 1500000000 | bytes 1000000 | tf_op jit(solution)/shard_map/split_heads/pallas_call | solution.py:54
  2.4 19.2 %all_to_all.10.qkv_ref.q_ref = bf16[8,480,128]{2,1,0:T(8,128)(2,1)S(1)} all-to-all(bf16[8,480,128]{2,1,0:T(8,128)(2,1)} %split_heads.1), channel_id=1, replica_groups=mesh['sup'=64,'core'=2,'grp'=4] {'core','grp'}, dimensions={0} | all-to-all | bytes 1966080 | tf_op jit(solution)/shard_map/all_to_all | solution.py:257
  21.6 0.0 copy-start
  21.6 3.8 %collective-permute-start.1 = (bf16[7,320,128]{2,1,0:T(8,128)(2,1)S(1)}, bf16[7,320,128]{2,1,0:T(8,128)(2,1)S(1)}, u32[]{:S(2)}, u32[]{:S(2)}) collective-permute-start(bf16[7,320,128]{2,1,0:T(8,128)(2,1)S(1)} %slice.8), channel_id=1, source_target_pairs={{0,8},{8,16},{16,24},{24,32},{32,40},{40,48},{48,56},{56,64},{64,7... | collective-permute-start | bytes 1720328 | tf_op jit(solution)/shard_map/ppermute | solution.py:253
  25.5 9.8 %collective-permute-start = (bf16[7,320,128]{2,1,0:T(8,128)(2,1)S(1)}, bf16[7,320,128]{2,1,0:T(8,128)(2,1)S(1)}, u32[]{:S(2)}, u32[]{:S(2)}) collective-permute-start(bf16[7,320,128]{2,1,0:T(8,128)(2,1)S(1)} %slice.7), channel_id=1, source_target_pairs={{8,0},{16,8},{24,16},{32,24},{40,32},{48,40},{56,48},{64,56},{72,6... | collective-permute-start | bytes 1720328 | tf_op jit(solution)/shard_map/ppermute | solution.py:253
  35.3 0.0 copy-done
  35.3 6.6 %own_part.1 = (bf16[8,160,128]{2,1,0:T(8,128)(2,1)S(1)}, f32[8,160,128]{2,1,0:T(8,128)S(1)}, f32[8,1,256]{2,1,0:T(1,128)S(1)}, f32[8,1,256]{2,1,0:T(1,128)S(1)}) custom-call(s32[512]{0:T(512)S(1)} %copy-done, bf16[8,480,128]{2,1,0:T(8,128)(2,1)S(1)} %all_to_all.10.qkv_ref.q_ref), custom_call_target="tpu_custom_call" | custom-call | flops 99999997952 | bytes 1000000 | tf_op jit(solution)/shard_map/own_part/pallas_call | solution.py:139
  41.9 4.7 %collective-permute-done.1.kv_ref = bf16[7,320,128]{2,1,0:T(8,128)(2,1)S(1)} collective-permute-done((bf16[7,320,128]{2,1,0:T(8,128)(2,1)S(1)}, bf16[7,320,128]{2,1,0:T(8,128)(2,1)S(1)}, u32[]{:S(2)}, u32[]{:S(2)}) %collective-permute-start.1) | collective-permute-done | bytes 573472 | tf_op jit(solution)/shard_map/ppermute | solution.py:253
  46.5 0.6 %halo_part.2.start_ref = bf16[8,160,128]{2,1,0:T(8,128)(2,1)S(1)} custom-call(s32[512]{0:T(512)S(1)} %copy-done, bf16[7,320,128]{2,1,0:T(8,128)(2,1)S(1)} %collective-permute-done.1.kv_ref, bf16[8,480,128]{2,1,0:T(8,128)(2,1)S(1)} %all_to_all.10.qkv_ref.q_ref, bf16[8,160,128]{2,1,0:T(8,128)(2,1)S(1)} %get-tuple-element.11.start_ref, ...), custom_call_target="tpu_custom_call" | custom-call | flops 1000000000 | bytes 1000000 | tf_op jit(solution)/shard_map/halo_part/pallas_call | solution.py:231
  47.2 0.6 %collective-permute-done.kv_ref = bf16[7,320,128]{2,1,0:T(8,128)(2,1)S(1)} collective-permute-done((bf16[7,320,128]{2,1,0:T(8,128)(2,1)S(1)}, bf16[7,320,128]{2,1,0:T(8,128)(2,1)S(1)}, u32[]{:S(2)}, u32[]{:S(2)}) %collective-permute-start) | collective-permute-done | bytes 573472 | tf_op jit(solution)/shard_map/ppermute | solution.py:253
  47.8 1.6 %halo_part.3 = bf16[8,160,128]{2,1,0:T(8,128)(2,1)S(1)} custom-call(s32[512]{0:T(512)S(1)} %copy-done, bf16[7,320,128]{2,1,0:T(8,128)(2,1)S(1)} %collective-permute-done.kv_ref, bf16[8,480,128]{2,1,0:T(8,128)(2,1)S(1)} %all_to_all.10.qkv_ref.q_ref, bf16[8,160,128]{2,1,0:T(8,128)(2,1)S(1)} %halo_part.2.start_ref, ...), custom_call_target="tpu_custom_call" | custom-call | flops 1000000000 | bytes 1000000 | tf_op jit(solution)/shard_map/halo_part/pallas_call | solution.py:231
  49.3 10.4 %all_to_all.11.in_ref = bf16[8,160,128]{2,1,0:T(8,128)(2,1)S(1)} all-to-all(bf16[8,160,128]{2,1,0:T(8,128)(2,1)S(1)} %halo_part.3), channel_id=1, replica_groups=mesh['sup'=64,'core'=2,'grp'=4] {'core','grp'}, dimensions={0} | all-to-all | bytes 655360 | tf_op jit(solution)/shard_map/all_to_all | solution.py:257
  59.7 0.9 %join_heads.1 = bf16[128,1280]{1,0:T(8,128)(2,1)} custom-call(bf16[8,160,128]{2,1,0:T(8,128)(2,1)S(1)} %all_to_all.11.in_ref), custom_call_target="tpu_custom_call" | custom-call | tf_op jit(solution)/shard_map/join_heads/pallas_call | solution.py:70
  (2 shorter events, 0.1 us)
Async XLA Ops:
  21.6 13.7 %copy-start = (s32[512]{0:T(512)S(1)}, s32[512]{0:T(512)}, u32[]{:S(2)}) copy-start(s32[512]{0:T(512)} %image_ref.5) | copy-start | bytes 6148
  21.6 24.9 %collective-permute-start.1 = (bf16[7,320,128]{2,1,0:T(8,128)(2,1)S(1)}, bf16[7,320,128]{2,1,0:T(8,128)(2,1)S(1)}, u32[]{:S(2)}, u32[]{:S(2)}) collective-permute-start(bf16[7,320,128]{2,1,0:T(8,128)(2,1)S(1)} %slice.8), channel_id=1, source_target_pairs={{0,8},{8,16},{16,24},{24,32},{32,40},{40,48},{48,56},{56,64},{64,7... | collective-permute-start | bytes 1720328 | tf_op jit(solution)/shard_map/ppermute | solution.py:253
  25.5 22.3 %collective-permute-start = (bf16[7,320,128]{2,1,0:T(8,128)(2,1)S(1)}, bf16[7,320,128]{2,1,0:T(8,128)(2,1)S(1)}, u32[]{:S(2)}, u32[]{:S(2)}) collective-permute-start(bf16[7,320,128]{2,1,0:T(8,128)(2,1)S(1)} %slice.7), channel_id=1, source_target_pairs={{8,0},{16,8},{24,16},{32,24},{40,32},{48,40},{56,48},{64,56},{72,6... | collective-permute-start | bytes 1720328 | tf_op jit(solution)/shard_map/ppermute | solution.py:253

commit v5 on v4

--- a/solution.py
+++ b/solution.py
@@ -157,21 +157,21 @@
     return how(values.reshape(BLK // 8, 8, 2 * BLK), axis=0)
 
 
-def halo_kernel(side, image_ref, kv_ref, q_ref, start_ref, acc_ref, max_ref, den_ref, out_ref, *scratch):
+def halo_kernel(turn, image_ref, kv_ref, q_ref, start_ref, acc_ref, max_ref, den_ref, out_ref, *scratch):
     keys, scores, tops, shifts, sums, dens = scratch
     place, places = lax.axis_index("sup"), lax.axis_size("sup")
+    from_below = lax.axis_index("core") == turn
     group = place * PER
-    if side == 0:
-        image, beyond = image_ref[group], jnp.maximum(group - (PER - 1), 0)
-        there = place > 0
-    else:
-        image, beyond = image_ref[group + PER - 1], jnp.minimum(group + PER, (places - 1) * PER)
-        there = place < places - 1
+    image = image_ref[jnp.where(from_below, group, group + PER - 1)]
+    beyond = jnp.where(
+        from_below, jnp.maximum(group - (PER - 1), 0), jnp.minimum(group + PER, (places - 1) * PER)
+    )
+    there = jnp.where(from_below, place > 0, place < places - 1)
     count = sum((there & (image_ref[beyond + j] == image)).astype(jnp.int32) for j in range(PER - 1))
     queries = sum((image_ref[group + j] == image).astype(jnp.int32) for j in range(PER))
     pairs = count * queries
-    first_query = 0 if side == 0 else PER - queries
-    first_key = PER - 1 - count if side == 0 else 0
+    first_query = jnp.where(from_below, 0, PER - queries)
+    first_key = jnp.where(from_below, PER - 1 - count, 0)
     steps = (pairs + STEP - 1) // STEP
 
     def advance(at):
@@ -198,7 +198,7 @@
                 tops[i] = jnp.maximum(tops[i], fold_rows(found, jnp.max))
             return at
 
-        start = (jnp.int32(first_query), jnp.int32(0))
+        start = (first_query, jnp.int32(0))
         lax.fori_loop(0, steps, look, start)
         for block in range(PER):
             shifts[block] = jnp.max(tops[block], axis=0, keepdims=True) * SCALE_LOG2
@@ -227,9 +227,9 @@
         lax.fori_loop(first_query, first_query + queries, close, 0)
 
 
-def halo_part(side, image, kv, q, start, acc, top, den):
-    return pl.pallas_call(
-        functools.partial(halo_kernel, side),
+def halo_part(turn, image, kv, q, start, acc, top, den):
+    return pl.pallas_call(
+        functools.partial(halo_kernel, turn),
         out_shape=jax.ShapeDtypeStruct((PER, WIDTH, BLK), BF16),
         in_specs=[SMEM] + [VMEM] * 6,
         out_specs=VMEM,
@@ -247,10 +247,19 @@
     )(image, kv, q, start, acc, top, den)
 
 
-def shifted(value, steps):
-    count = lax.axis_size("sup")
-    pairs = [(i, i + steps) for i in range(count) if 0 <= i + steps < count]
-    return lax.ppermute(value, "sup", pairs)
+def exchanged(qkv, turn):
+    groups, cores = lax.axis_size("sup"), lax.axis_size("core")
+    pairs = []
+    for core in range(cores):
+        step = 1 if core == turn else -1
+        pairs += [
+            (group * cores + core, (group + step) * cores + core)
+            for group in range(groups)
+            if 0 <= group + step < groups
+        ]
+    first = (lax.axis_index("core") == turn).astype(jnp.int32)
+    part = lax.dynamic_slice(qkv, (first, WIDTH, 0), (PER - 1, 2 * WIDTH, BLK))
+    return part, lax.ppermute(part, ("sup", "core"), pairs)
 
 
 def regrouped(parts):
@@ -259,13 +268,12 @@
 
 def body(query_rows, key_rows, value_rows, block_image):
     qkv = regrouped(split_heads(query_rows, key_rows, value_rows))
-    rising = qkv[1:, WIDTH:]
-    below = shifted(rising, 1)
-    qkv, rising = lax.optimization_barrier((qkv, rising))
-    above = shifted(qkv[:-1, WIDTH:], -1)
+    part, near = exchanged(qkv, 0)
+    again, part = lax.optimization_barrier((qkv, part))
+    part, far = exchanged(again, 1)
     start, acc, top, den = own_part(block_image, qkv)
-    result = halo_part(0, block_image, below, qkv, start, acc, top, den)
-    result = halo_part(1, block_image, above, qkv, result, acc, top, den)
+    result = halo_part(0, block_image, near, qkv, start, acc, top, den)
+    result = halo_part(1, block_image, far, qkv, result, acc, top, den)
     return join_heads(regrouped(result))
 
 

time: 61.3 us -> 60.8 us (level)
  blocking collectives: 29.5 us -> 11.6 us
  waiting for transfers between devices: 5.3 us -> 17.1 us
  starting transfers between devices: 13.6 us -> 18.1 us
  Pallas kernels: 12 us -> 12.9 us
    all_to_all x2 -> x1, blocking collectives: 29.5 us -> 11.6 us  [regrouped(): return lax.all_to_all(parts, ('core', 'grp'), 0, 0, tiled=True)]
    all_to_all x0 -> x1, waiting for transfers between devices: none -> 14.6 us  [regrouped(): return lax.all_to_all(parts, ('core', 'grp'), 0, 0, tiled=True)]
    all_to_all x0 -> x1, starting transfers between devices: none -> 4.48 us  [regrouped(): return lax.all_to_all(parts, ('core', 'grp'), 0, 0, tiled=True)]
    ppermute x2, waiting for transfers between devices: 5.3 us -> 2.46 us  [exchanged(): return (part, lax.ppermute(part, ('sup', 'core'), pairs))]
    pallas_call x2, Pallas kernels: 2.16 us -> 3.14 us  [halo_part(): pl.pallas_call(functools.partial(halo_kernel, turn), out_shape=jax.ShapeD...]
  transfers between devices with their start and end apart: 2 -> 3, of which waited for: 2 -> 3; matrix products, arithmetic and copies ran while one was open for 0% -> 0% of each run, Pallas kernels for 12% -> 13%
where the time goes in v5:
time: 60.8 us; the launch traced here: 59.8 us
  starting transfers between devices  18.1 us (30%)
  waiting for transfers between devices  17.1 us (28%)
  Pallas kernels  12.9 us (21%)
  blocking collectives  11.6 us (19%)
    all_to_all x1, waiting for transfers between devices, regrouped(): return lax.all_to_all(parts, ('core', 'grp'), 0, 0, tiled=True)  14.6 us
    ppermute x2, starting transfers between devices, exchanged(): return (part, lax.ppermute(part, ('sup', 'core'), pairs))  13.6 us
    all_to_all x1, blocking collectives, regrouped(): return lax.all_to_all(parts, ('core', 'grp'), 0, 0, tiled=True)  11.6 us
    pallas_call x1, Pallas kernels, own_part(): pl.pallas_call(own_kernel, out_shape=(jax.ShapeDtypeStruct((PER, WIDTH, B...  6.48 us
    all_to_all x1, starting transfers between devices, regrouped(): return lax.all_to_all(parts, ('core', 'grp'), 0, 0, tiled=True)  4.48 us
    pallas_call x2, Pallas kernels, halo_part(): pl.pallas_call(functools.partial(halo_kernel, turn), out_shape=jax.ShapeD...  3.14 us
    ppermute x2, waiting for transfers between devices, exchanged(): return (part, lax.ppermute(part, ('sup', 'core'), pairs))  2.46 us
    pallas_call x1, Pallas kernels, split_heads(): pl.pallas_call(split_kernel, out_shape=jax.ShapeDtypeStruct((PER, WIDTH *...  2.37 us
  transfers between devices with their start and end apart: 3, of which 3 were waited for; matrix products, arithmetic and copies ran while one was open for 0% of the time, Pallas kernels for 13%

profile of v5, /device:TPU:6, one launch (start us, length us, event | category | flops | bytes accessed | tf_op | source)
XLA Modules:
  0.0 59.8 jit_solution(16546074019170387246)
XLA Ops:
  0.0 2.4 %split_heads.1 = bf16[8,480,128]{2,1,0:T(8,128)(2,1)} custom-call(bf16[128,1280]{1,0:T(8,128)(2,1)} %refs_0_.1, bf16[128,1280]{1,0:T(8,128)(2,1)} %refs_1_.1, bf16[128,1280]{1,0:T(8,128)(2,1)} %refs_2_.1), custom_call_target="tpu_custom_call" | custom-call | flops 1500000000 | bytes 1000000 | tf_op jit(solution)/shard_map/split_heads/pallas_call | solution.py:54
  2.4 4.5 %all-to-all-start = ((bf16[8,480,128]{2,1,0:T(8,128)(2,1)}), bf16[8,480,128]{2,1,0:T(8,128)(2,1)S(1)}, u32[]{:S(2)}, u32[]{:S(2)}) async-start(bf16[8,480,128]{2,1,0:T(8,128)(2,1)} %split_heads.1), calls=%async_computation | async-start | bytes 1966080 | tf_op jit(solution)/shard_map/all_to_all | solution.py:266
  6.9 14.6 %all-to-all-done.qkv_ref.q_ref = bf16[8,480,128]{2,1,0:T(8,128)(2,1)S(1)} async-done(((bf16[8,480,128]{2,1,0:T(8,128)(2,1)}), bf16[8,480,128]{2,1,0:T(8,128)(2,1)S(1)}, u32[]{:S(2)}, u32[]{:S(2)}) %all-to-all-start) | async-done | bytes 983072 | tf_op jit(solution)/shard_map/all_to_all | solution.py:266
  21.5 0.0 copy-start
  21.6 3.8 %collective-permute-start.1 = (bf16[7,320,128]{2,1,0:T(8,128)(2,1)S(1)}, bf16[7,320,128]{2,1,0:T(8,128)(2,1)S(1)}, u32[]{:S(2)}, u32[]{:S(2)}) collective-permute-start(bf16[7,320,128]{2,1,0:T(8,128)(2,1)S(1)} %constant_dynamic-slice_fusion.1), channel_id=1, source_target_pairs={{0,8},{8,16},{16,24},{24,32},{32,40},{40,48},{48,56},{56,64},{64,7... | collective-permute-start | bytes 1720328 | tf_op jit(solution)/shard_map/ppermute | solution.py:262
  25.4 9.8 %collective-permute-start = (bf16[7,320,128]{2,1,0:T(8,128)(2,1)S(1)}, bf16[7,320,128]{2,1,0:T(8,128)(2,1)S(1)}, u32[]{:S(2)}, u32[]{:S(2)}) collective-permute-start(bf16[7,320,128]{2,1,0:T(8,128)(2,1)S(1)} %constant_dynamic-slice_fusion), channel_id=1, source_target_pairs={{8,0},{16,8},{24,16},{32,24},{40,32},{48,40},{56,48},{64,56},{72,6... | collective-permute-start | bytes 1720328 | tf_op jit(solution)/shard_map/ppermute | solution.py:262
  35.2 0.0 copy-done
  35.2 6.5 %own_part.1 = (bf16[8,160,128]{2,1,0:T(8,128)(2,1)S(1)}, f32[8,160,128]{2,1,0:T(8,128)S(1)}, f32[8,1,256]{2,1,0:T(1,128)S(1)}, f32[8,1,256]{2,1,0:T(1,128)S(1)}) custom-call(s32[512]{0:T(512)S(1)} %copy-done, bf16[8,480,128]{2,1,0:T(8,128)(2,1)S(1)} %all-to-all-done.qkv_ref.q_ref), custom_call_target="tpu_custom_call" | custom-call | flops 99999997952 | bytes 1000000 | tf_op jit(solution)/shard_map/own_part/pallas_call | solution.py:139
  41.7 0.3 collective-permute-done.1.kv_ref
  42.0 1.6 %halo_part.2.start_ref = bf16[8,160,128]{2,1,0:T(8,128)(2,1)S(1)} custom-call(s32[512]{0:T(512)S(1)} %copy-done, bf16[7,320,128]{2,1,0:T(8,128)(2,1)S(1)} %collective-permute-done.1.kv_ref, bf16[8,480,128]{2,1,0:T(8,128)(2,1)S(1)} %all-to-all-done.qkv_ref.q_ref, bf16[8,160,128]{2,1,0:T(8,128)(2,1)S(1)} %get-tuple-element.11.start_ref, ...), custom_call_target="tpu_custom_call" | custom-call | flops 1000000000 | bytes 1000000 | tf_op jit(solution)/shard_map/halo_part/pallas_call | solution.py:231
  43.6 2.2 %collective-permute-done.kv_ref = bf16[7,320,128]{2,1,0:T(8,128)(2,1)S(1)} collective-permute-done((bf16[7,320,128]{2,1,0:T(8,128)(2,1)S(1)}, bf16[7,320,128]{2,1,0:T(8,128)(2,1)S(1)}, u32[]{:S(2)}, u32[]{:S(2)}) %collective-permute-start) | collective-permute-done | bytes 573472 | tf_op jit(solution)/shard_map/ppermute | solution.py:262
  45.8 1.6 %halo_part.3 = bf16[8,160,128]{2,1,0:T(8,128)(2,1)S(1)} custom-call(s32[512]{0:T(512)S(1)} %copy-done, bf16[7,320,128]{2,1,0:T(8,128)(2,1)S(1)} %collective-permute-done.kv_ref, bf16[8,480,128]{2,1,0:T(8,128)(2,1)S(1)} %all-to-all-done.qkv_ref.q_ref, bf16[8,160,128]{2,1,0:T(8,128)(2,1)S(1)} %halo_part.2.start_ref, ...), custom_call_target="tpu_custom_call" | custom-call | flops 1000000000 | bytes 1000000 | tf_op jit(solution)/shard_map/halo_part/pallas_call | solution.py:231
  47.3 11.6 %all_to_all.10.in_ref = bf16[8,160,128]{2,1,0:T(8,128)(2,1)S(1)} all-to-all(bf16[8,160,128]{2,1,0:T(8,128)(2,1)S(1)} %halo_part.3), channel_id=1, replica_groups=mesh['sup'=64,'core'=2,'grp'=4] {'core','grp'}, dimensions={0} | all-to-all | bytes 655360 | tf_op jit(solution)/shard_map/all_to_all | solution.py:266
  58.9 0.9 %join_heads.1 = bf16[128,1280]{1,0:T(8,128)(2,1)} custom-call(bf16[8,160,128]{2,1,0:T(8,128)(2,1)S(1)} %all_to_all.10.in_ref), custom_call_target="tpu_custom_call" | custom-call | tf_op jit(solution)/shard_map/join_heads/pallas_call | solution.py:70
  (2 shorter events, 0.1 us)
Async XLA Ops:
  2.4 19.1 %all-to-all-start = ((bf16[8,480,128]{2,1,0:T(8,128)(2,1)}), bf16[8,480,128]{2,1,0:T(8,128)(2,1)S(1)}, u32[]{:S(2)}, u32[]{:S(2)}) async-start(bf16[8,480,128]{2,1,0:T(8,128)(2,1)} %split_heads.1), calls=%async_computation | async-start | bytes 1966080 | tf_op jit(solution)/shard_map/all_to_all | solution.py:266
  21.5 13.7 %copy-start = (s32[512]{0:T(512)S(1)}, s32[512]{0:T(512)}, u32[]{:S(2)}) copy-start(s32[512]{0:T(512)} %image_ref.5) | copy-start | bytes 6148
  21.6 20.4 %collective-permute-start.1 = (bf16[7,320,128]{2,1,0:T(8,128)(2,1)S(1)}, bf16[7,320,128]{2,1,0:T(8,128)(2,1)S(1)}, u32[]{:S(2)}, u32[]{:S(2)}) collective-permute-start(bf16[7,320,128]{2,1,0:T(8,128)(2,1)S(1)} %constant_dynamic-slice_fusion.1), channel_id=1, source_target_pairs={{0,8},{8,16},{16,24},{24,32},{32,40},{40,48},{48,56},{56,64},{64,7... | collective-permute-start | bytes 1720328 | tf_op jit(solution)/shard_map/ppermute | solution.py:262
  25.4 20.3 %collective-permute-start = (bf16[7,320,128]{2,1,0:T(8,128)(2,1)S(1)}, bf16[7,320,128]{2,1,0:T(8,128)(2,1)S(1)}, u32[]{:S(2)}, u32[]{:S(2)}) collective-permute-start(bf16[7,320,128]{2,1,0:T(8,128)(2,1)S(1)} %constant_dynamic-slice_fusion), channel_id=1, source_target_pairs={{8,0},{16,8},{24,16},{32,24},{40,32},{48,40},{56,48},{64,56},{72,6... | collective-permute-start | bytes 1720328 | tf_op jit(solution)/shard_map/ppermute | solution.py:262

commit v6 on v5

--- a/solution.py
+++ b/solution.py
@@ -57,9 +57,10 @@
         in_specs=[HBM] * count,
         out_specs=VMEM,
         scratch_shapes=[pltpu.VMEM((count, BLK, PER * WIDTH), BF16), pltpu.SemaphoreType.DMA((count,))],
+        compiler_params=pltpu.CompilerParams(vmem_limit_bytes=49152 * 1024),
         cost_estimate=cost(500_000_000 * count),
         name="split_heads",
-    )(*arrays)
+    )(*[pltpu.with_memory_space_constraint(a, pltpu.HBM) for a in arrays])
 
 
 def join_kernel(in_ref, out_ref):
@@ -247,6 +248,23 @@
     )(image, kv, q, start, acc, top, den)
 
 
+def pick_kernel(turn, qkv_ref, out_ref):
+    first = (lax.axis_index("core") == turn).astype(jnp.int32)
+    out_ref[...] = qkv_ref[pl.ds(first, PER - 1), WIDTH:, :]
+
+
+def picked(qkv, turn):
+    return pl.pallas_call(
+        functools.partial(pick_kernel, turn),
+        out_shape=jax.ShapeDtypeStruct((PER - 1, 2 * WIDTH, BLK), BF16),
+        in_specs=[VMEM],
+        out_specs=VMEM,
+        compiler_params=LIMIT,
+        cost_estimate=cost(1_000_000),
+        name="picked",
+    )(qkv)
+
+
 def exchanged(qkv, turn):
     groups, cores = lax.axis_size("sup"), lax.axis_size("core")
     pairs = []
@@ -257,8 +275,7 @@
             for group in range(groups)
             if 0 <= group + step < groups
         ]
-    first = (lax.axis_index("core") == turn).astype(jnp.int32)
-    part = lax.dynamic_slice(qkv, (first, WIDTH, 0), (PER - 1, 2 * WIDTH, BLK))
+    part = picked(qkv, turn)
     return part, lax.ppermute(part, ("sup", "core"), pairs)
 
 

time: 60.8 us -> 59.8 us (0.984)
  blocking collectives: 11.6 us -> 31.2 us
  waiting for transfers between devices: 17.1 us -> 1.67 us
  starting transfers between devices: 18.1 us -> 13.6 us
    all_to_all x1 -> x2, blocking collectives: 11.6 us -> 31.2 us  [regrouped(): return lax.all_to_all(parts, ('core', 'grp'), 0, 0, tiled=True)]
    all_to_all x1 -> x0, waiting for transfers between devices: 14.6 us -> none  [regrouped(): return lax.all_to_all(parts, ('core', 'grp'), 0, 0, tiled=True)]
    all_to_all x1 -> x0, starting transfers between devices: 4.48 us -> none  [regrouped(): return lax.all_to_all(parts, ('core', 'grp'), 0, 0, tiled=True)]
    pallas_call x1, Pallas kernels: 2.37 us -> 1.42 us  [split_heads(): pl.pallas_call(split_kernel, out_shape=jax.ShapeDtypeStruct((PER, WIDTH *...]
    ppermute x2, waiting for transfers between devices: 2.46 us -> 1.67 us  [exchanged(): return (part, lax.ppermute(part, ('sup', 'core'), pairs))]
    pallas_call x2, Pallas kernels: 3.14 us -> 3.85 us  [halo_part(): pl.pallas_call(functools.partial(halo_kernel, turn), out_shape=jax.ShapeD...]
  transfers between devices with their start and end apart: 3 -> 2, of which waited for: 3 -> 2; matrix products, arithmetic and copies ran while one was open for 0% -> 0% of each run, Pallas kernels for 13% -> 15%
where the time goes in v6:
time: 59.8 us; the launch traced here: 59.3 us
  blocking collectives  31.2 us (52%)
  starting transfers between devices  13.6 us (23%)
  Pallas kernels  12.7 us (21%)
  waiting for transfers between devices  1.67 us (3%)
    all_to_all x2, blocking collectives, regrouped(): return lax.all_to_all(parts, ('core', 'grp'), 0, 0, tiled=True)  31.2 us
    ppermute x2, starting transfers between devices, exchanged(): return (part, lax.ppermute(part, ('sup', 'core'), pairs))  13.6 us
    pallas_call x1, Pallas kernels, own_part(): pl.pallas_call(own_kernel, out_shape=(jax.ShapeDtypeStruct((PER, WIDTH, B...  6.52 us
    pallas_call x2, Pallas kernels, halo_part(): pl.pallas_call(functools.partial(halo_kernel, turn), out_shape=jax.ShapeD...  3.85 us
    ppermute x2, waiting for transfers between devices, exchanged(): return (part, lax.ppermute(part, ('sup', 'core'), pairs))  1.67 us
    pallas_call x1, Pallas kernels, split_heads(): pl.pallas_call(split_kernel, out_shape=jax.ShapeDtypeStruct((PER, WIDTH *...  1.42 us
  transfers between devices with their start and end apart: 2, of which 2 were waited for; matrix products, arithmetic and copies ran while one was open for 0% of the time, Pallas kernels for 15%

profile of v6, /device:TPU:6, one launch (start us, length us, event | category | flops | bytes accessed | tf_op | source)
XLA Modules:
  0.0 59.3 jit_solution(2991867285283271684)
XLA Ops:
  0.0 1.4 %split_heads.1 = bf16[8,480,128]{2,1,0:T(8,128)(2,1)S(1)} custom-call(bf16[128,1280]{1,0:T(8,128)(2,1)} %refs_0_.1, bf16[128,1280]{1,0:T(8,128)(2,1)} %refs_1_.1, bf16[128,1280]{1,0:T(8,128)(2,1)} %refs_2_.1), custom_call_target="tpu_custom_call" | custom-call | flops 1500000000 | bytes 1000000 | tf_op jit(solution)/shard_map/split_heads/pallas_call | solution.py:54
  1.4 19.0 %all_to_all.10.qkv_ref.q_ref = bf16[8,480,128]{2,1,0:T(8,128)(2,1)S(1)} all-to-all(bf16[8,480,128]{2,1,0:T(8,128)(2,1)S(1)} %split_heads.1), channel_id=1, replica_groups=mesh['sup'=64,'core'=2,'grp'=4] {'core','grp'}, dimensions={0} | all-to-all | bytes 1966080 | tf_op jit(solution)/shard_map/all_to_all | solution.py:283
  20.4 0.0 copy-start
  20.5 3.8 %collective-permute-start.1 = (bf16[7,320,128]{2,1,0:T(8,128)(2,1)S(1)}, bf16[7,320,128]{2,1,0:T(8,128)(2,1)S(1)}, u32[]{:S(2)}, u32[]{:S(2)}) collective-permute-start(bf16[7,320,128]{2,1,0:T(8,128)(2,1)S(1)} %picked.2), channel_id=1, source_target_pairs={{0,8},{8,16},{16,24},{24,32},{32,40},{40,48},{48,56},{56,64},{64,7... | collective-permute-start | bytes 1720328 | tf_op jit(solution)/shard_map/ppermute | solution.py:279
  24.3 0.1 picked.3
  24.3 9.8 %collective-permute-start = (bf16[7,320,128]{2,1,0:T(8,128)(2,1)S(1)}, bf16[7,320,128]{2,1,0:T(8,128)(2,1)S(1)}, u32[]{:S(2)}, u32[]{:S(2)}) collective-permute-start(bf16[7,320,128]{2,1,0:T(8,128)(2,1)S(1)} %picked.3), channel_id=1, source_target_pairs={{8,0},{16,8},{24,16},{32,24},{40,32},{48,40},{56,48},{64,56},{72,6... | collective-permute-start | bytes 1720328 | tf_op jit(solution)/shard_map/ppermute | solution.py:279
  34.1 0.0 copy-done
  34.1 6.5 %own_part.1 = (bf16[8,160,128]{2,1,0:T(8,128)(2,1)S(1)}, f32[8,160,128]{2,1,0:T(8,128)S(1)}, f32[8,1,256]{2,1,0:T(1,128)S(1)}, f32[8,1,256]{2,1,0:T(1,128)S(1)}) custom-call(s32[512]{0:T(512)S(1)} %copy-done, bf16[8,480,128]{2,1,0:T(8,128)(2,1)S(1)} %all_to_all.10.qkv_ref.q_ref), custom_call_target="tpu_custom_call" | custom-call | flops 99999997952 | bytes 1000000 | tf_op jit(solution)/shard_map/own_part/pallas_call | solution.py:140
  40.7 0.3 collective-permute-done.1.kv_ref
  40.9 2.3 %halo_part.2.start_ref = bf16[8,160,128]{2,1,0:T(8,128)(2,1)S(1)} custom-call(s32[512]{0:T(512)S(1)} %copy-done, bf16[7,320,128]{2,1,0:T(8,128)(2,1)S(1)} %collective-permute-done.1.kv_ref, bf16[8,480,128]{2,1,0:T(8,128)(2,1)S(1)} %all_to_all.10.qkv_ref.q_ref, bf16[8,160,128]{2,1,0:T(8,128)(2,1)S(1)} %get-tuple-element.11.start_ref, ...), custom_call_target="tpu_custom_call" | custom-call | flops 1000000000 | bytes 1000000 | tf_op jit(solution)/shard_map/halo_part/pallas_call | solution.py:232
  43.2 1.4 %collective-permute-done.kv_ref = bf16[7,320,128]{2,1,0:T(8,128)(2,1)S(1)} collective-permute-done((bf16[7,320,128]{2,1,0:T(8,128)(2,1)S(1)}, bf16[7,320,128]{2,1,0:T(8,128)(2,1)S(1)}, u32[]{:S(2)}, u32[]{:S(2)}) %collective-permute-start) | collective-permute-done | bytes 573472 | tf_op jit(solution)/shard_map/ppermute | solution.py:279
  44.6 1.6 %halo_part.3 = bf16[8,160,128]{2,1,0:T(8,128)(2,1)S(1)} custom-call(s32[512]{0:T(512)S(1)} %copy-done, bf16[7,320,128]{2,1,0:T(8,128)(2,1)S(1)} %collective-permute-done.kv_ref, bf16[8,480,128]{2,1,0:T(8,128)(2,1)S(1)} %all_to_all.10.qkv_ref.q_ref, bf16[8,160,128]{2,1,0:T(8,128)(2,1)S(1)} %halo_part.2.start_ref, ...), custom_call_target="tpu_custom_call" | custom-call | flops 1000000000 | bytes 1000000 | tf_op jit(solution)/shard_map/halo_part/pallas_call | solution.py:232
  46.2 12.3 %all_to_all.11.in_ref = bf16[8,160,128]{2,1,0:T(8,128)(2,1)S(1)} all-to-all(bf16[8,160,128]{2,1,0:T(8,128)(2,1)S(1)} %halo_part.3), channel_id=1, replica_groups=mesh['sup'=64,'core'=2,'grp'=4] {'core','grp'}, dimensions={0} | all-to-all | bytes 655360 | tf_op jit(solution)/shard_map/all_to_all | solution.py:283
  58.5 0.9 %join_heads.1 = bf16[128,1280]{1,0:T(8,128)(2,1)} custom-call(bf16[8,160,128]{2,1,0:T(8,128)(2,1)S(1)} %all_to_all.11.in_ref), custom_call_target="tpu_custom_call" | custom-call | tf_op jit(solution)/shard_map/join_heads/pallas_call | solution.py:71
  (1 shorter events, 0.0 us)
Async XLA Ops:
  20.4 13.7 %copy-start = (s32[512]{0:T(512)S(1)}, s32[512]{0:T(512)}, u32[]{:S(2)}) copy-start(s32[512]{0:T(512)} %image_ref.5) | copy-start | bytes 6148
  20.5 20.5 %collective-permute-start.1 = (bf16[7,320,128]{2,1,0:T(8,128)(2,1)S(1)}, bf16[7,320,128]{2,1,0:T(8,128)(2,1)S(1)}, u32[]{:S(2)}, u32[]{:S(2)}) collective-permute-start(bf16[7,320,128]{2,1,0:T(8,128)(2,1)S(1)} %picked.2), channel_id=1, source_target_pairs={{0,8},{8,16},{16,24},{24,32},{32,40},{40,48},{48,56},{56,64},{64,7... | collective-permute-start | bytes 1720328 | tf_op jit(solution)/shard_map/ppermute | solution.py:279
  24.3 20.3 %collective-permute-start = (bf16[7,320,128]{2,1,0:T(8,128)(2,1)S(1)}, bf16[7,320,128]{2,1,0:T(8,128)(2,1)S(1)}, u32[]{:S(2)}, u32[]{:S(2)}) collective-permute-start(bf16[7,320,128]{2,1,0:T(8,128)(2,1)S(1)} %picked.3), channel_id=1, source_target_pairs={{8,0},{16,8},{24,16},{32,24},{40,32},{48,40},{56,48},{64,56},{72,6... | collective-permute-start | bytes 1720328 | tf_op jit(solution)/shard_map/ppermute | solution.py:279

commit v7 on v6

--- a/solution.py
+++ b/solution.py
@@ -18,6 +18,7 @@
 FAR = 1e30
 SLOTS = 16
 STEP = 8
+RUN = 16
 VMEM = pl.BlockSpec(memory_space=pltpu.VMEM)
 SMEM = pl.BlockSpec(memory_space=pltpu.SMEM)
 HBM = pl.BlockSpec(memory_space=pltpu.HBM)
@@ -30,16 +31,17 @@
     return pl.CostEstimate(flops=flops, bytes_accessed=1_000_000, transcendentals=0)
 
 
-def split_kernel(*refs):
-    count = len(refs) - 3
-    sources, out_ref, held, sems = refs[:count], refs[count], refs[count + 1], refs[count + 2]
+def split_kernel(counts, *refs):
+    count, outs = sum(counts), len(counts)
+    sources, out_refs, (held, sems) = refs[:count], refs[count : count + outs], refs[count + outs :]
     copies = [pltpu.make_async_copy(ref, held.at[place], sems.at[place]) for place, ref in enumerate(sources)]
     for copy in copies:
         copy.start()
-    for place, copy in enumerate(copies):
-        copy.wait()
+    places = [(out_ref, place) for out_ref, many in zip(out_refs, counts) for place in range(many)]
+    for source, (out_ref, place) in enumerate(places):
+        copies[source].wait()
         for tile in range(TILES):
-            turned = held[place, :, tile * BLK : (tile + 1) * BLK].T
+            turned = held[source, :, tile * BLK : (tile + 1) * BLK].T
             first = tile * BLK
             while first < (tile + 1) * BLK:
                 part, row = divmod(first, WIDTH)
@@ -49,18 +51,22 @@
                 first += size
 
 
-def split_heads(*arrays):
-    count = len(arrays)
-    return pl.pallas_call(
-        split_kernel,
-        out_shape=jax.ShapeDtypeStruct((PER, WIDTH * count, BLK), BF16),
-        in_specs=[HBM] * count,
-        out_specs=VMEM,
-        scratch_shapes=[pltpu.VMEM((count, BLK, PER * WIDTH), BF16), pltpu.SemaphoreType.DMA((count,))],
+def split_heads(*groups):
+    arrays = [pltpu.with_memory_space_constraint(array, pltpu.HBM) for group in groups for array in group]
+    counts = tuple(len(group) for group in groups)
+    return pl.pallas_call(
+        functools.partial(split_kernel, counts),
+        out_shape=[jax.ShapeDtypeStruct((PER, WIDTH * count, BLK), BF16) for count in counts],
+        in_specs=[HBM] * len(arrays),
+        out_specs=[VMEM] * len(counts),
+        scratch_shapes=[
+            pltpu.VMEM((len(arrays), BLK, PER * WIDTH), BF16),
+            pltpu.SemaphoreType.DMA((len(arrays),)),
+        ],
         compiler_params=pltpu.CompilerParams(vmem_limit_bytes=49152 * 1024),
-        cost_estimate=cost(500_000_000 * count),
+        cost_estimate=cost(500_000_000 * len(arrays)),
         name="split_heads",
-    )(*[pltpu.with_memory_space_constraint(a, pltpu.HBM) for a in arrays])
+    )(*arrays)
 
 
 def join_kernel(in_ref, out_ref):
@@ -98,45 +104,68 @@
     )
 
 
-def own_kernel(image_ref, qkv_ref, out_ref, acc_ref, max_ref, den_ref, keys, scores):
+def fold_rows(values, how):
+    return how(values.reshape(BLK // 8, 8, 2 * BLK), axis=0)
+
+
+def own_kernel(image_ref, kv_ref, q_ref, out_ref, acc_ref, max_ref, den_ref, *scratch):
+    bounds, keys, scores, tops, shifts, dens = scratch
+    group = lax.axis_index("sup") * PER
+    pairs = jnp.int32(0)
     for block in range(PER):
-        keys[block * BLK : (block + 1) * BLK, :] = qkv_ref[block, WIDTH : 2 * WIDTH, :].T
-
-    group = lax.axis_index("sup") * PER
-
-    def one(i, carry):
-        image = image_ref[group + i]
+        image = image_ref[group + block]
         first = sum((image_ref[group + j] < image).astype(jnp.int32) for j in range(PER))
         last = sum((image_ref[group + j] <= image).astype(jnp.int32) for j in range(PER))
-        weights_in = both_heads(qkv_ref[i, :WIDTH, :])
-        top = jnp.full((1, 2 * BLK), -FAR, F32)
-        for j in range(PER):
-            rows = slice(j * BLK, (j + 1) * BLK)
-            found = jnp.dot(keys[rows, :], weights_in, preferred_element_type=F32)
-            scores[rows, :] = found
-            inside = (j >= first) & (j < last)
-            top = jnp.maximum(top, jnp.where(inside, jnp.max(found, axis=0, keepdims=True), -FAR))
-        shift = top * SCALE_LOG2
-        total = jnp.zeros((WIDTH, 2 * BLK), F32)
-        den = jnp.zeros((1, 2 * BLK), F32)
-        for j in range(PER):
-            rows = slice(j * BLK, (j + 1) * BLK)
-            inside = (j >= first) & (j < last)
-            here = jnp.where(inside, shift, FAR)
-            weights = jnp.exp2(scores[rows, :] * SCALE_LOG2 - here)
-            den += jnp.sum(weights, axis=0, keepdims=True)
-            total += jnp.dot(qkv_ref[j, 2 * WIDTH :, :], weights.astype(BF16), preferred_element_type=F32)
-        acc = diagonal(total)
-        acc_ref[i] = acc
-        max_ref[i] = top
-        den_ref[i] = den
-        out_ref[i] = (acc * per_row(1.0 / den)).astype(BF16)
-        return carry
-
-    lax.fori_loop(0, PER, one, 0)
-
-
-def own_part(image, qkv):
+        bounds[0, block] = first
+        bounds[1, block] = last
+        pairs += last - first
+        keys[block] = kv_ref[block, :WIDTH, :].T
+    steps = (pairs + STEP - 1) // STEP
+    tops[...] = jnp.full_like(tops, -FAR)
+    dens[...] = jnp.zeros_like(dens)
+    acc_ref[...] = jnp.zeros_like(acc_ref)
+
+    def advance(at):
+        i, j = at
+        wrap = j + 1 == bounds[1, i]
+        i = jnp.where(wrap, jnp.minimum(i + 1, PER - 1), i)
+        return i, jnp.where(wrap, bounds[0, i], j + 1)
+
+    def look(step, at):
+        for lane in range(STEP):
+            i, j = at
+            at = advance(at)
+            found = jnp.dot(keys[j], both_heads(q_ref[i]), preferred_element_type=F32)
+            scores[step * STEP + lane] = found
+            tops[i] = jnp.maximum(tops[i], fold_rows(found, jnp.max))
+        return at
+
+    start = (jnp.int32(0), jnp.int32(0))
+    lax.fori_loop(0, steps, look, start)
+    for block in range(PER):
+        top = jnp.max(tops[block], axis=0, keepdims=True)
+        max_ref[block] = top
+        shifts[block] = top * SCALE_LOG2
+
+    def weigh(step, at):
+        for lane in range(STEP):
+            pair = step * STEP + lane
+            i, j = at
+            at = advance(at)
+            shift = jnp.where(pair < pairs, shifts[i], FAR)
+            weights = jnp.exp2(scores[pair] * SCALE_LOG2 - shift)
+            dens[i] += fold_rows(weights, jnp.sum)
+            acc_ref[i] += diagonal(jnp.dot(kv_ref[j, WIDTH:, :], weights.astype(BF16), preferred_element_type=F32))
+        return at
+
+    lax.fori_loop(0, steps, weigh, start)
+    for block in range(PER):
+        den = jnp.sum(dens[block], axis=0, keepdims=True)
+        den_ref[block] = den
+        out_ref[block] = (acc_ref[block] * per_row(1.0 / den)).astype(BF16)
+
+
+def own_part(image, kv, q):
     return pl.pallas_call(
         own_kernel,
         out_shape=(
@@ -145,17 +174,20 @@
             jax.ShapeDtypeStruct((PER, 1, 2 * BLK), F32),
             jax.ShapeDtypeStruct((PER, 1, 2 * BLK), F32),
         ),
-        in_specs=[SMEM, VMEM],
+        in_specs=[SMEM, VMEM, VMEM],
         out_specs=(VMEM,) * 4,
-        scratch_shapes=[pltpu.VMEM((PER * BLK, WIDTH), BF16), pltpu.VMEM((PER * BLK, 2 * BLK), F32)],
+        scratch_shapes=[
+            pltpu.SMEM((2, PER), jnp.int32),
+            pltpu.VMEM((PER, BLK, WIDTH), BF16),
+            pltpu.VMEM((PER * PER, BLK, 2 * BLK), F32),
+            pltpu.VMEM((PER, 8, 2 * BLK), F32),
+            pltpu.VMEM((PER, 1, 2 * BLK), F32),
+            pltpu.VMEM((PER, 8, 2 * BLK), F32),
+        ],
         compiler_params=LIMIT,
         cost_estimate=cost(100_000_000_000),
         name="own_part",
-    )(image, qkv)
-
-
-def fold_rows(values, how):
-    return how(values.reshape(BLK // 8, 8, 2 * BLK), axis=0)
+    )(image, kv, q)
 
 
 def halo_kernel(turn, image_ref, kv_ref, q_ref, start_ref, acc_ref, max_ref, den_ref, out_ref, *scratch):
@@ -194,7 +226,7 @@
                 pair = step * STEP + lane
                 i, j = at[0], first_key + at[1]
                 at = advance(at)
-                found = jnp.dot(keys[j], both_heads(q_ref[i, :WIDTH, :]), preferred_element_type=F32)
+                found = jnp.dot(keys[j], both_heads(q_ref[i]), preferred_element_type=F32)
                 scores[pair] = found
                 tops[i] = jnp.maximum(tops[i], fold_rows(found, jnp.max))
             return at
@@ -248,12 +280,12 @@
     )(image, kv, q, start, acc, top, den)
 
 
-def pick_kernel(turn, qkv_ref, out_ref):
+def pick_kernel(turn, kv_ref, out_ref):
     first = (lax.axis_index("core") == turn).astype(jnp.int32)
-    out_ref[...] = qkv_ref[pl.ds(first, PER - 1), WIDTH:, :]
-
-
-def picked(qkv, turn):
+    out_ref[...] = kv_ref[pl.ds(first, PER - 1)]
+
+
+def picked(kv, turn):
     return pl.pallas_call(
         functools.partial(pick_kernel, turn),
         out_shape=jax.ShapeDtypeStruct((PER - 1, 2 * WIDTH, BLK), BF16),
@@ -262,10 +294,10 @@
         compiler_params=LIMIT,
         cost_estimate=cost(1_000_000),
         name="picked",
-    )(qkv)
-
-
-def exchanged(qkv, turn):
+    )(kv)
+
+
+def exchanged(kv, turn):
     groups, cores = lax.axis_size("sup"), lax.axis_size("core")
     pairs = []
     for core in range(cores):
@@ -275,7 +307,7 @@
             for group in range(groups)
             if 0 <= group + step < groups
         ]
-    part = picked(qkv, turn)
+    part = picked(kv, turn)
     return part, lax.ppermute(part, ("sup", "core"), pairs)
 
 
@@ -284,13 +316,26 @@
 
 
 def body(query_rows, key_rows, value_rows, block_image):
-    qkv = regrouped(split_heads(query_rows, key_rows, value_rows))
-    part, near = exchanged(qkv, 0)
-    again, part = lax.optimization_barrier((qkv, part))
+    late = lax.rem(lax.axis_index("sup"), RUN) == RUN - 1
+
+    def together(query_rows, key_rows, value_rows):
+        (slabs,) = split_heads((query_rows, key_rows, value_rows))
+        qkv = regrouped(slabs)
+        return qkv[:, WIDTH:], qkv[:, :WIDTH]
+
+    def keys_first(query_rows, key_rows, value_rows):
+        slabs, q = split_heads((key_rows, value_rows), (query_rows,))
+        return regrouped(slabs), q
+
+    kv, q = lax.cond(late, keys_first, together, query_rows, key_rows, value_rows)
+    part, near = exchanged(kv, 0)
+    again, part = lax.optimization_barrier((kv, part))
     part, far = exchanged(again, 1)
-    start, acc, top, den = own_part(block_image, qkv)
-    result = halo_part(0, block_image, near, qkv, start, acc, top, den)
-    result = halo_part(1, block_image, far, qkv, result, acc, top, den)
+    part, q = lax.optimization_barrier((part, q))
+    q = lax.cond(late, regrouped, lambda q: q, q)
+    start, acc, top, den = own_part(block_image, kv, q)
+    result = halo_part(0, block_image, near, q, start, acc, top, den)
+    result = halo_part(1, block_image, far, q, result, acc, top, den)
     return join_heads(regrouped(result))
 
 

time: 59.8 us -> 55.9 us (0.935)
  the two profiles are of different devices: /device:TPU:6 before, /device:TPU:257 now
where the time goes in v7:
time: 55.9 us; the launch traced here: 55.6 us
  blocking collectives  32.2 us (58%)
  Pallas kernels  10.6 us (19%)
  waiting for transfers between devices  6.73 us (12%)
  starting transfers between devices  5.28 us (9%)
  local copies, waits for them, and re-layouts  0.73 us (1%)
    all_to_all x2, blocking collectives, regrouped(): return lax.all_to_all(parts, ('core', 'grp'), 0, 0, tiled=True)  32.2 us
    ppermute x2, waiting for transfers between devices, exchanged(): return (part, lax.ppermute(part, ('sup', 'core'), pairs))  6.73 us
    ppermute x2, starting transfers between devices, exchanged(): return (part, lax.ppermute(part, ('sup', 'core'), pairs))  5.28 us
    pallas_call x2, Pallas kernels, halo_part(): pl.pallas_call(functools.partial(halo_kernel, turn), out_shape=jax.ShapeD...  4.67 us
    pallas_call x1, Pallas kernels, own_part(): pl.pallas_call(own_kernel, out_shape=(jax.ShapeDtypeStruct((PER, WIDTH, B...  3.55 us
    pallas_call x1, Pallas kernels, split_heads(): pl.pallas_call(functools.partial(split_kernel, counts), out_shape=[jax.Sh...  1.42 us
  transfers between devices with their start and end apart: 2, of which 2 were waited for; matrix products, arithmetic and copies ran while one was open for 0% of the time, Pallas kernels for 11%

profile of v7, /device:TPU:257, one launch (start us, length us, event | category | flops | bytes accessed | tf_op | source)
XLA Modules:
  0.0 55.6 jit_solution(17310368726167517767)
XLA Ops:
  0.0 20.8 %conditional.2 = (bf16[8,320,128]{2,1,0:T(8,128)(2,1)S(1)}, bf16[8,160,128]{2,1,0:T(8,128)(2,1)S(1)}) conditional(s32[]{:T(128)} %convert_element_type.4, (bf16[128,1280]{1,0:T(8,128)(2,1)}, bf16[128,1280]{1,0:T(8,128)(2,1)}, bf16[128,1280]{1,0:T(8,128)(2,1)}) %tuple.21, (bf16[128,1280]{1,0:T(8,128)(2,1)}, bf16[128,1280]{1,0:T(8,128)(2,1)}, ...), branch_computations={%region_0.0_spmd, %region_1.0_spmd} | conditional | flops 1500000000 | bytes 4932176 | solution.py:330
  0.0 1.4 %split_heads.2 = bf16[8,480,128]{2,1,0:T(8,128)(2,1)S(1)} custom-call(bf16[128,1280]{1,0:T(8,128)(2,1)} %get-tuple-element.22.refs_0_, bf16[128,1280]{1,0:T(8,128)(2,1)} %get-tuple-element.23.refs_1_, bf16[128,1280]{1,0:T(8,128)(2,1)} %get-tuple-element.24.refs_2_), custom_call_target="tpu_custom_call" | custom-call | flops 1500000000 | bytes 1000000 | tf_op jit(solution)/shard_map/cond/branch_0_fun/split_heads/pallas_call | solution.py:57
  1.4 19.3 %all_to_all.17 = bf16[8,480,128]{2,1,0:T(8,128)(2,1)S(1)} all-to-all(bf16[8,480,128]{2,1,0:T(8,128)(2,1)S(1)} %split_heads.2), channel_id=1, replica_groups=mesh['sup'=64,'core'=2,'grp'=4] {'core','grp'}, dimensions={0} | all-to-all | bytes 1966080 | tf_op jit(solution)/shard_map/cond/branch_0_fun/all_to_all | solution.py:315
  20.8 0.1 picked.2
  20.8 1.9 %collective-permute-start.1 = (bf16[7,320,128]{2,1,0:T(8,128)(2,1)S(1)}, bf16[7,320,128]{2,1,0:T(8,128)(2,1)S(1)}, u32[]{:S(2)}, u32[]{:S(2)}) collective-permute-start(bf16[7,320,128]{2,1,0:T(8,128)(2,1)S(1)} %picked.2), channel_id=1, source_target_pairs={{0,8},{8,16},{16,24},{24,32},{32,40},{40,48},{48,56},{56,64},{64,7... | collective-permute-start | bytes 1720328 | tf_op jit(solution)/shard_map/ppermute | solution.py:311
  22.8 0.1 picked.3
  22.8 3.4 %collective-permute-start = (bf16[7,320,128]{2,1,0:T(8,128)(2,1)S(1)}, bf16[7,320,128]{2,1,0:T(8,128)(2,1)S(1)}, u32[]{:S(2)}, u32[]{:S(2)}) collective-permute-start(bf16[7,320,128]{2,1,0:T(8,128)(2,1)S(1)} %picked.3), channel_id=1, source_target_pairs={{8,0},{16,8},{24,16},{32,24},{40,32},{48,40},{56,48},{64,56},{72,6... | collective-permute-start | bytes 1720328 | tf_op jit(solution)/shard_map/ppermute | solution.py:311
  26.2 0.0 copy-start
  26.2 0.7 %copy-done = s32[512]{0:T(512)S(1)} copy-done((s32[512]{0:T(512)S(1)}, s32[512]{0:T(512)}, u32[]{:S(2)}) %copy-start) | copy-done | bytes 2072
  26.9 3.6 %own_part.1 = (bf16[8,160,128]{2,1,0:T(8,128)(2,1)S(1)}, f32[8,160,128]{2,1,0:T(8,128)S(1)}, f32[8,1,256]{2,1,0:T(1,128)S(1)}, f32[8,1,256]{2,1,0:T(1,128)S(1)}) custom-call(s32[512]{0:T(512)S(1)} %copy-done, bf16[8,320,128]{2,1,0:T(8,128)(2,1)S(1)} %get-tuple-element.39.kv_ref, bf16[8,160,128]{2,1,0:T(8,128)(2,1)S(1)} %get-tuple-element.50.q_ref), custom_call_target="tpu_custom_call" | custom-call | flops 99999997952 | bytes 1000000 | tf_op jit(solution)/shard_map/own_part/pallas_call | solution.py:169
  30.4 3.4 %collective-permute-done.1.kv_ref = bf16[7,320,128]{2,1,0:T(8,128)(2,1)S(1)} collective-permute-done((bf16[7,320,128]{2,1,0:T(8,128)(2,1)S(1)}, bf16[7,320,128]{2,1,0:T(8,128)(2,1)S(1)}, u32[]{:S(2)}, u32[]{:S(2)}) %collective-permute-start.1) | collective-permute-done | bytes 573472 | tf_op jit(solution)/shard_map/ppermute | solution.py:311
  33.8 2.3 %halo_part.2.start_ref = bf16[8,160,128]{2,1,0:T(8,128)(2,1)S(1)} custom-call(s32[512]{0:T(512)S(1)} %copy-done, bf16[7,320,128]{2,1,0:T(8,128)(2,1)S(1)} %collective-permute-done.1.kv_ref, bf16[8,160,128]{2,1,0:T(8,128)(2,1)S(1)} %get-tuple-element.50.q_ref, bf16[8,160,128]{2,1,0:T(8,128)(2,1)S(1)} %get-tuple-element.42.start_ref, ...), custom_call_target="tpu_custom_call" | custom-call | flops 1000000000 | bytes 1000000 | tf_op jit(solution)/shard_map/halo_part/pallas_call | solution.py:264
  36.1 3.4 %collective-permute-done.kv_ref = bf16[7,320,128]{2,1,0:T(8,128)(2,1)S(1)} collective-permute-done((bf16[7,320,128]{2,1,0:T(8,128)(2,1)S(1)}, bf16[7,320,128]{2,1,0:T(8,128)(2,1)S(1)}, u32[]{:S(2)}, u32[]{:S(2)}) %collective-permute-start) | collective-permute-done | bytes 573472 | tf_op jit(solution)/shard_map/ppermute | solution.py:311
  39.5 2.4 %halo_part.3 = bf16[8,160,128]{2,1,0:T(8,128)(2,1)S(1)} custom-call(s32[512]{0:T(512)S(1)} %copy-done, bf16[7,320,128]{2,1,0:T(8,128)(2,1)S(1)} %collective-permute-done.kv_ref, bf16[8,160,128]{2,1,0:T(8,128)(2,1)S(1)} %get-tuple-element.50.q_ref, bf16[8,160,128]{2,1,0:T(8,128)(2,1)S(1)} %halo_part.2.start_ref, ...), custom_call_target="tpu_custom_call" | custom-call | flops 1000000000 | bytes 1000000 | tf_op jit(solution)/shard_map/halo_part/pallas_call | solution.py:264
  41.8 12.9 %all_to_all.20.in_ref = bf16[8,160,128]{2,1,0:T(8,128)(2,1)S(1)} all-to-all(bf16[8,160,128]{2,1,0:T(8,128)(2,1)S(1)} %halo_part.3), channel_id=1, replica_groups=mesh['sup'=64,'core'=2,'grp'=4] {'core','grp'}, dimensions={0} | all-to-all | bytes 655360 | tf_op jit(solution)/shard_map/all_to_all | solution.py:315
  54.7 0.9 %join_heads.1 = bf16[128,1280]{1,0:T(8,128)(2,1)} custom-call(bf16[8,160,128]{2,1,0:T(8,128)(2,1)S(1)} %all_to_all.20.in_ref), custom_call_target="tpu_custom_call" | custom-call | tf_op jit(solution)/shard_map/join_heads/pallas_call | solution.py:77
  (3 shorter events, 0.1 us)
Async XLA Ops:
  20.8 13.0 %collective-permute-start.1 = (bf16[7,320,128]{2,1,0:T(8,128)(2,1)S(1)}, bf16[7,320,128]{2,1,0:T(8,128)(2,1)S(1)}, u32[]{:S(2)}, u32[]{:S(2)}) collective-permute-start(bf16[7,320,128]{2,1,0:T(8,128)(2,1)S(1)} %picked.2), channel_id=1, source_target_pairs={{0,8},{8,16},{16,24},{24,32},{32,40},{40,48},{48,56},{56,64},{64,7... | collective-permute-start | bytes 1720328 | tf_op jit(solution)/shard_map/ppermute | solution.py:311
  22.8 16.7 %collective-permute-start = (bf16[7,320,128]{2,1,0:T(8,128)(2,1)S(1)}, bf16[7,320,128]{2,1,0:T(8,128)(2,1)S(1)}, u32[]{:S(2)}, u32[]{:S(2)}) collective-permute-start(bf16[7,320,128]{2,1,0:T(8,128)(2,1)S(1)} %picked.3), channel_id=1, source_target_pairs={{8,0},{16,8},{24,16},{32,24},{40,32},{48,40},{56,48},{64,56},{72,6... | collective-permute-start | bytes 1720328 | tf_op jit(solution)/shard_map/ppermute | solution.py:311
  26.2 0.7 %copy-start = (s32[512]{0:T(512)S(1)}, s32[512]{0:T(512)}, u32[]{:S(2)}) copy-start(s32[512]{0:T(512)} %image_ref.5) | copy-start | bytes 6148

commit v8 on v7

--- a/solution.py
+++ b/solution.py
@@ -19,6 +19,7 @@
 SLOTS = 16
 STEP = 8
 RUN = 16
+FEW = 4
 VMEM = pl.BlockSpec(memory_space=pltpu.VMEM)
 SMEM = pl.BlockSpec(memory_space=pltpu.SMEM)
 HBM = pl.BlockSpec(memory_space=pltpu.HBM)
@@ -29,6 +30,10 @@
 
 def cost(flops):
     return pl.CostEstimate(flops=flops, bytes_accessed=1_000_000, transcendentals=0)
+
+
+def is_late():
+    return lax.rem(lax.axis_index("sup"), RUN) >= FEW
 
 
 def split_kernel(counts, *refs):
@@ -202,7 +207,7 @@
     there = jnp.where(from_below, place > 0, place < places - 1)
     count = sum((there & (image_ref[beyond + j] == image)).astype(jnp.int32) for j in range(PER - 1))
     queries = sum((image_ref[group + j] == image).astype(jnp.int32) for j in range(PER))
-    pairs = count * queries
+    pairs = jnp.where(is_late(), 0, count * queries)
     first_query = jnp.where(from_below, 0, PER - queries)
     first_key = jnp.where(from_below, PER - 1 - count, 0)
     steps = (pairs + STEP - 1) // STEP
@@ -278,6 +283,124 @@
         cost_estimate=cost(1_000_000_000),
         name="halo_part",
     )(image, kv, q, start, acc, top, den)
+
+
+def all_kernel(image_ref, kv_ref, near_ref, far_ref, q_ref, out_ref, *scratch):
+    bounds, keys, values, scores, tops, shifts, dens, sums = scratch
+    place, places = lax.axis_index("sup"), lax.axis_size("sup")
+    group = place * PER
+    side = PER - 1
+
+    def held(first, ref):
+        for block in range(ref.shape[0]):
+            keys[first + block] = ref[block, :WIDTH, :].T
+            values[first + block] = ref[block, WIDTH:, :]
+
+    held(side, kv_ref)
+
+    @pl.when(lax.axis_index("core") == 0)
+    def _():
+        held(0, near_ref)
+        held(side + PER, far_ref)
+
+    @pl.when(lax.axis_index("core") != 0)
+    def _():
+        held(0, far_ref)
+        held(side + PER, near_ref)
+
+    lowest, highest = image_ref[group], image_ref[group + PER - 1]
+    below, above = jnp.maximum(group - side, 0), jnp.minimum(group + PER, (places - 1) * PER)
+    more_below = sum(((place > 0) & (image_ref[below + j] == lowest)).astype(jnp.int32) for j in range(side))
+    more_above = sum(
+        ((place < places - 1) & (image_ref[above + j] == highest)).astype(jnp.int32) for j in range(side)
+    )
+    pairs = jnp.int32(0)
+    for block in range(PER):
+        image = image_ref[group + block]
+        first = side + sum((image_ref[group + j] < image).astype(jnp.int32) for j in range(PER))
+        last = side + sum((image_ref[group + j] <= image).astype(jnp.int32) for j in range(PER))
+        first -= jnp.where(image == lowest, more_below, 0)
+        last += jnp.where(image == highest, more_above, 0)
+        bounds[0, block] = first
+        bounds[1, block] = last
+        pairs += last - first
+    steps = (pairs + STEP - 1) // STEP
+    tops[...] = jnp.full_like(tops, -FAR)
+    dens[...] = jnp.zeros_like(dens)
+    sums[...] = jnp.zeros_like(sums)
+
+    def advance(at):
+        i, j = at
+        wrap = j + 1 == bounds[1, i]
+        i = jnp.where(wrap, jnp.minimum(i + 1, PER - 1), i)
+        return i, jnp.where(wrap, bounds[0, i], j + 1)
+
+    def look(step, at):
+        for lane in range(STEP):
+            i, j = at
+            at = advance(at)
+            found = jnp.dot(keys[j], both_heads(q_ref[i]), preferred_element_type=F32)
+            scores[step * STEP + lane] = found
+            tops[i] = jnp.maximum(tops[i], fold_rows(found, jnp.max))
+        return at
+
+    start = (jnp.int32(0), bounds[0, 0])
+    lax.fori_loop(0, steps, look, start)
+    for block in range(PER):
+        shifts[block] = jnp.max(tops[block], axis=0, keepdims=True) * SCALE_LOG2
+
+    def weigh(step, at):
+        for lane in range(STEP):
+            pair = step * STEP + lane
+            i, j = at
+            at = advance(at)
+            shift = jnp.where(pair < pairs, shifts[i], FAR)
+            weights = jnp.exp2(scores[pair] * SCALE_LOG2 - shift)
+            dens[i] += fold_rows(weights, jnp.sum)
+            sums[i] += diagonal(jnp.dot(values[j], weights.astype(BF16), preferred_element_type=F32))
+        return at
+
+    lax.fori_loop(0, steps, weigh, start)
+    for block in range(PER):
+        den = jnp.sum(dens[block], axis=0, keepdims=True)
+        out_ref[block] = (sums[block] * per_row(1.0 / den)).astype(BF16)
+
+
+def last_kernel(image_ref, kv_ref, near_ref, far_ref, q_ref, start_ref, acc_ref, max_ref, den_ref, out_ref, *scratch):
+    bounds, keys, values, scores, tops, shifts, dens, sums = scratch
+    late = is_late()
+
+    @pl.when(late)
+    def _():
+        all_kernel(image_ref, kv_ref, near_ref, far_ref, q_ref, out_ref, *scratch)
+
+    @pl.when(jnp.logical_not(late))
+    def _():
+        rest = (keys, scores, tops, shifts, sums, dens)
+        halo_kernel(1, image_ref, far_ref, q_ref, start_ref, acc_ref, max_ref, den_ref, out_ref, *rest)
+
+
+def last_part(image, kv, near, far, q, start, acc, top, den):
+    blocks = 3 * PER - 2
+    return pl.pallas_call(
+        last_kernel,
+        out_shape=jax.ShapeDtypeStruct((PER, WIDTH, BLK), BF16),
+        in_specs=[SMEM] + [VMEM] * 8,
+        out_specs=VMEM,
+        scratch_shapes=[
+            pltpu.SMEM((2, PER), jnp.int32),
+            pltpu.VMEM((blocks, BLK, WIDTH), BF16),
+            pltpu.VMEM((blocks, WIDTH, BLK), BF16),
+            pltpu.VMEM((PER * PER, BLK, 2 * BLK), F32),
+            pltpu.VMEM((PER, 8, 2 * BLK), F32),
+            pltpu.VMEM((PER, 1, 2 * BLK), F32),
+            pltpu.VMEM((PER, 8, 2 * BLK), F32),
+            pltpu.VMEM((PER, WIDTH, BLK), F32),
+        ],
+        compiler_params=LIMIT,
+        cost_estimate=cost(1_000_000_000),
+        name="last_part",
+    )(image, kv, near, far, q, start, acc, top, den)
 
 
 def pick_kernel(turn, kv_ref, out_ref):
@@ -316,7 +439,7 @@
 
 
 def body(query_rows, key_rows, value_rows, block_image):
-    late = lax.rem(lax.axis_index("sup"), RUN) == RUN - 1
+    late = is_late()
 
     def together(query_rows, key_rows, value_rows):
         (slabs,) = split_heads((query_rows, key_rows, value_rows))
@@ -332,10 +455,17 @@
     again, part = lax.optimization_barrier((kv, part))
     part, far = exchanged(again, 1)
     part, q = lax.optimization_barrier((part, q))
-    q = lax.cond(late, regrouped, lambda q: q, q)
-    start, acc, top, den = own_part(block_image, kv, q)
+
+    def own_now(kv, q):
+        return q, *own_part(block_image, kv, q)
+
+    def queries_now(kv, q):
+        stat = jnp.zeros((PER, 1, 2 * BLK), F32)
+        return regrouped(q), jnp.zeros((PER, WIDTH, BLK), BF16), jnp.zeros((PER, WIDTH, BLK), F32), stat, stat
+
+    q, start, acc, top, den = lax.cond(late, queries_now, own_now, kv, q)
     result = halo_part(0, block_image, near, q, start, acc, top, den)
-    result = halo_part(1, block_image, far, q, result, acc, top, den)
+    result = last_part(block_image, kv, near, far, q, result, acc, top, den)
     return join_heads(regrouped(result))
 
 

time: 55.9 us -> 56.2 us (level)
  the two profiles are of different devices: /device:TPU:257 before, /device:TPU:6 now
where the time goes in v8:
time: 56.2 us; the launch traced here: 55.2 us
  blocking collectives  31.6 us (56%)
  starting transfers between devices  9.96 us (18%)
  Pallas kernels  7.57 us (13%)
  waiting for transfers between devices  5.9 us (10%)
    all_to_all x2, blocking collectives, regrouped(): return lax.all_to_all(parts, ('core', 'grp'), 0, 0, tiled=True)  31.6 us
    ppermute x2, starting transfers between devices, exchanged(): return (part, lax.ppermute(part, ('sup', 'core'), pairs))  9.96 us
    ppermute x2, waiting for transfers between devices, exchanged(): return (part, lax.ppermute(part, ('sup', 'core'), pairs))  5.9 us
    pallas_call x1, Pallas kernels, own_part(): pl.pallas_call(own_kernel, out_shape=(jax.ShapeDtypeStruct((PER, WIDTH, B...  2.89 us
    pallas_call x1, Pallas kernels, halo_part(): pl.pallas_call(functools.partial(halo_kernel, turn), out_shape=jax.ShapeD...  1.67 us
    pallas_call x1, Pallas kernels, split_heads(): pl.pallas_call(functools.partial(split_kernel, counts), out_shape=[jax.Sh...  1.42 us
  transfers between devices with their start and end apart: 2, of which 2 were waited for; matrix products, arithmetic and copies ran while one was open for 0% of the time, Pallas kernels for 8%

profile of v8, /device:TPU:6, one launch (start us, length us, event | category | flops | bytes accessed | tf_op | source)
XLA Modules:
  0.0 55.2 jit_solution(12619666930775849828)
XLA Ops:
  0.0 20.5 %conditional.2 = (bf16[8,320,128]{2,1,0:T(8,128)(2,1)S(1)}, bf16[8,160,128]{2,1,0:T(8,128)(2,1)S(1)}) conditional(s32[]{:T(128)} %convert_element_type.4, (bf16[128,1280]{1,0:T(8,128)(2,1)}, bf16[128,1280]{1,0:T(8,128)(2,1)}, bf16[128,1280]{1,0:T(8,128)(2,1)}) %tuple.23, (bf16[128,1280]{1,0:T(8,128)(2,1)}, bf16[128,1280]{1,0:T(8,128)(2,1)}, ...), branch_computations={%region_0.0_spmd, %region_1.0_spmd} | conditional | flops 1500000000 | bytes 4932176 | solution.py:453
  0.0 1.4 %split_heads.2 = bf16[8,480,128]{2,1,0:T(8,128)(2,1)S(1)} custom-call(bf16[128,1280]{1,0:T(8,128)(2,1)} %get-tuple-element.24.refs_0_, bf16[128,1280]{1,0:T(8,128)(2,1)} %get-tuple-element.25.refs_1_, bf16[128,1280]{1,0:T(8,128)(2,1)} %get-tuple-element.26.refs_2_), custom_call_target="tpu_custom_call" | custom-call | flops 1500000000 | bytes 1000000 | tf_op jit(solution)/shard_map/cond/branch_0_fun/split_heads/pallas_call | solution.py:62
  1.4 19.0 %all_to_all.17 = bf16[8,480,128]{2,1,0:T(8,128)(2,1)S(1)} all-to-all(bf16[8,480,128]{2,1,0:T(8,128)(2,1)S(1)} %split_heads.2), channel_id=1, replica_groups=mesh['sup'=64,'core'=2,'grp'=4] {'core','grp'}, dimensions={0} | all-to-all | bytes 1966080 | tf_op jit(solution)/shard_map/cond/branch_0_fun/all_to_all | solution.py:438
  20.5 0.1 picked.2
  20.5 0.0 copy-start
  20.6 3.8 %collective-permute-start = (bf16[7,320,128]{2,1,0:T(8,128)(2,1)S(1)}, bf16[7,320,128]{2,1,0:T(8,128)(2,1)S(1)}, u32[]{:S(2)}, u32[]{:S(2)}) collective-permute-start(bf16[7,320,128]{2,1,0:T(8,128)(2,1)S(1)} %picked.2), channel_id=1, source_target_pairs={{0,8},{8,16},{16,24},{24,32},{32,40},{40,48},{48,56},{56,64},{64,7... | collective-permute-start | bytes 1720328 | tf_op jit(solution)/shard_map/ppermute | solution.py:434
  24.4 0.1 picked.3
  24.5 6.1 %collective-permute-start.1 = (bf16[7,320,128]{2,1,0:T(8,128)(2,1)S(1)}, bf16[7,320,128]{2,1,0:T(8,128)(2,1)S(1)}, u32[]{:S(2)}, u32[]{:S(2)}) collective-permute-start(bf16[7,320,128]{2,1,0:T(8,128)(2,1)S(1)} %picked.3), channel_id=1, source_target_pairs={{8,0},{16,8},{24,16},{32,24},{40,32},{48,40},{56,48},{64,56},{72,6... | collective-permute-start | bytes 1720328 | tf_op jit(solution)/shard_map/ppermute | solution.py:434
  30.6 0.0 copy-done
  30.6 2.9 %conditional.3 = (bf16[8,160,128]{2,1,0:T(8,128)(2,1)S(1)}, bf16[8,160,128]{2,1,0:T(8,128)(2,1)S(1)}, f32[8,160,128]{2,1,0:T(8,128)S(1)}, f32[8,1,256]{2,1,0:T(1,128)S(1)}, f32[8,1,256]{2,1,0:T(1,128)S(1)}) conditional(s32[]{:T(128)} %convert_element_type.4, (s32[512]{0:T(512)S(1)}, bf16[8,320,128]{2,1,0:T(8,128)(2,1)S(1)}, ...), branch_computations={%region_2.0_spmd, %region_3.0_spmd} | conditional | flops 99999997952 | bytes 2310198 | solution.py:466
  30.6 2.9 %own_part.1 = (bf16[8,160,128]{2,1,0:T(8,128)(2,1)S(1)}, f32[8,160,128]{2,1,0:T(8,128)S(1)}, f32[8,1,256]{2,1,0:T(1,128)S(1)}, f32[8,1,256]{2,1,0:T(1,128)S(1)}) custom-call(s32[512]{0:T(512)S(1)} %get-tuple-element.33.image_ref, bf16[8,320,128]{2,1,0:T(8,128)(2,1)S(1)} %get-tuple-element.34.kv_ref, bf16[8,160,128]{2,1,0:T(8,128)(2,1)S(1)} %get-tuple-element.61.q_ref), custom_call_target="tpu_custom_call" | custom-call | flops 99999997952 | bytes 1000000 | tf_op jit(solution)/shard_map/cond/branch_0_fun/own_part/pallas_call | solution.py:174
  33.5 3.9 %collective-permute-done.kv_ref.near_ref = bf16[7,320,128]{2,1,0:T(8,128)(2,1)S(1)} collective-permute-done((bf16[7,320,128]{2,1,0:T(8,128)(2,1)S(1)}, bf16[7,320,128]{2,1,0:T(8,128)(2,1)S(1)}, u32[]{:S(2)}, u32[]{:S(2)}) %collective-permute-start) | collective-permute-done | bytes 573472 | tf_op jit(solution)/shard_map/ppermute | solution.py:434
  37.4 1.7 %halo_part.1.start_ref = bf16[8,160,128]{2,1,0:T(8,128)(2,1)S(1)} custom-call(s32[512]{0:T(512)S(1)} %copy-done, bf16[7,320,128]{2,1,0:T(8,128)(2,1)S(1)} %collective-permute-done.kv_ref.near_ref, bf16[8,160,128]{2,1,0:T(8,128)(2,1)S(1)} %get-tuple-element.52.q_ref, bf16[8,160,128]{2,1,0:T(8,128)(2,1)S(1)} %get-tuple-element.53.start_ref, ...), custom_call_target="tpu_custom_call" | custom-call | flops 1000000000 | bytes 1000000 | tf_op jit(solution)/shard_map/halo_part/pallas_call | solution.py:269
  39.1 2.0 %collective-permute-done.1.far_ref = bf16[7,320,128]{2,1,0:T(8,128)(2,1)S(1)} collective-permute-done((bf16[7,320,128]{2,1,0:T(8,128)(2,1)S(1)}, bf16[7,320,128]{2,1,0:T(8,128)(2,1)S(1)}, u32[]{:S(2)}, u32[]{:S(2)}) %collective-permute-start.1) | collective-permute-done | bytes 573472 | tf_op jit(solution)/shard_map/ppermute | solution.py:434
  41.1 0.6 %last_part.1 = bf16[8,160,128]{2,1,0:T(8,128)(2,1)S(1)} custom-call(s32[512]{0:T(512)S(1)} %copy-done, bf16[8,320,128]{2,1,0:T(8,128)(2,1)S(1)} %get-tuple-element.49.kv_ref, bf16[7,320,128]{2,1,0:T(8,128)(2,1)S(1)} %collective-permute-done.kv_ref.near_ref, bf16[7,320,128]{2,1,0:T(8,128)(2,1)S(1)} %collective-permute-done.1.far_ref, ...), custom_call_target="tpu_custom_call" | custom-call | flops 1000000000 | bytes 1000000 | tf_op jit(solution)/shard_map/last_part/pallas_call | solution.py:385
  41.7 12.6 %all_to_all.20.in_ref = bf16[8,160,128]{2,1,0:T(8,128)(2,1)S(1)} all-to-all(bf16[8,160,128]{2,1,0:T(8,128)(2,1)S(1)} %last_part.1), channel_id=1, replica_groups=mesh['sup'=64,'core'=2,'grp'=4] {'core','grp'}, dimensions={0} | all-to-all | bytes 655360 | tf_op jit(solution)/shard_map/all_to_all | solution.py:438
  54.3 0.9 %join_heads.1 = bf16[128,1280]{1,0:T(8,128)(2,1)} custom-call(bf16[8,160,128]{2,1,0:T(8,128)(2,1)S(1)} %all_to_all.20.in_ref), custom_call_target="tpu_custom_call" | custom-call | tf_op jit(solution)/shard_map/join_heads/pallas_call | solution.py:82
  (2 shorter events, 0.1 us)
Async XLA Ops:
  20.5 10.0 %copy-start = (s32[512]{0:T(512)S(1)}, s32[512]{0:T(512)}, u32[]{:S(2)}) copy-start(s32[512]{0:T(512)} %image_ref.3) | copy-start | bytes 6148
  20.6 16.8 %collective-permute-start = (bf16[7,320,128]{2,1,0:T(8,128)(2,1)S(1)}, bf16[7,320,128]{2,1,0:T(8,128)(2,1)S(1)}, u32[]{:S(2)}, u32[]{:S(2)}) collective-permute-start(bf16[7,320,128]{2,1,0:T(8,128)(2,1)S(1)} %picked.2), channel_id=1, source_target_pairs={{0,8},{8,16},{16,24},{24,32},{32,40},{40,48},{48,56},{56,64},{64,7... | collective-permute-start | bytes 1720328 | tf_op jit(solution)/shard_map/ppermute | solution.py:434
  24.5 16.6 %collective-permute-start.1 = (bf16[7,320,128]{2,1,0:T(8,128)(2,1)S(1)}, bf16[7,320,128]{2,1,0:T(8,128)(2,1)S(1)}, u32[]{:S(2)}, u32[]{:S(2)}) collective-permute-start(bf16[7,320,128]{2,1,0:T(8,128)(2,1)S(1)} %picked.3), channel_id=1, source_target_pairs={{8,0},{16,8},{24,16},{32,24},{40,32},{48,40},{56,48},{64,56},{72,6... | collective-permute-start | bytes 1720328 | tf_op jit(solution)/shard_map/ppermute | solution.py:434

commit v9 on v8

--- a/solution.py
+++ b/solution.py
@@ -18,6 +18,7 @@
 FAR = 1e30
 SLOTS = 16
 STEP = 8
+WIDE = 16
 RUN = 16
 FEW = 4
 VMEM = pl.BlockSpec(memory_space=pltpu.VMEM)
@@ -210,7 +211,6 @@
     pairs = jnp.where(is_late(), 0, count * queries)
     first_query = jnp.where(from_below, 0, PER - queries)
     first_key = jnp.where(from_below, PER - 1 - count, 0)
-    steps = (pairs + STEP - 1) // STEP
 
     def advance(at):
         i, j = at
@@ -226,9 +226,8 @@
         for block in range(PER):
             tops[block] = jnp.broadcast_to(max_ref[block], (8, 2 * BLK))
 
-        def look(step, at):
-            for lane in range(STEP):
-                pair = step * STEP + lane
+        def look(lanes, at):
+            for pair in range(lanes):
                 i, j = at[0], first_key + at[1]
                 at = advance(at)
                 found = jnp.dot(keys[j], both_heads(q_ref[i]), preferred_element_type=F32)
@@ -237,15 +236,22 @@
             return at
 
         start = (first_query, jnp.int32(0))
-        lax.fori_loop(0, steps, look, start)
+
+        @pl.when(pairs <= STEP)
+        def _():
+            look(STEP, start)
+
+        @pl.when(pairs > STEP)
+        def _():
+            look(SLOTS, start)
+
         for block in range(PER):
             shifts[block] = jnp.max(tops[block], axis=0, keepdims=True) * SCALE_LOG2
         sums[...] = jnp.zeros_like(sums)
         dens[...] = jnp.zeros_like(dens)
 
-        def weigh(step, at):
-            for lane in range(STEP):
-                pair = step * STEP + lane
+        def weigh(lanes, at):
+            for pair in range(lanes):
                 i, j = at[0], first_key + at[1]
                 at = advance(at)
                 shift = jnp.where(pair < pairs, shifts[i], FAR)
@@ -254,7 +260,15 @@
                 sums[i] += diagonal(jnp.dot(kv_ref[j, WIDTH:, :], weights.astype(BF16), preferred_element_type=F32))
             return at
 
-        lax.fori_loop(0, steps, weigh, start)
+
+        @pl.when(pairs <= STEP)
+        def _():
+            weigh(STEP, start)
+
+        @pl.when(pairs > STEP)
+        def _():
+            weigh(SLOTS, start)
+
 
         def close(i, carry):
             fade = jnp.exp2(max_ref[i] * SCALE_LOG2 - shifts[i])
@@ -324,7 +338,7 @@
         bounds[0, block] = first
         bounds[1, block] = last
         pairs += last - first
-    steps = (pairs + STEP - 1) // STEP
+    steps = (pairs + WIDE - 1) // WIDE
     tops[...] = jnp.full_like(tops, -FAR)
     dens[...] = jnp.zeros_like(dens)
     sums[...] = jnp.zeros_like(sums)
@@ -336,11 +350,11 @@
         return i, jnp.where(wrap, bounds[0, i], j + 1)
 
     def look(step, at):
-        for lane in range(STEP):
+        for lane in range(WIDE):
             i, j = at
             at = advance(at)
             found = jnp.dot(keys[j], both_heads(q_ref[i]), preferred_element_type=F32)
-            scores[step * STEP + lane] = found
+            scores[step * WIDE + lane] = found
             tops[i] = jnp.maximum(tops[i], fold_rows(found, jnp.max))
         return at
 
@@ -350,8 +364,8 @@
         shifts[block] = jnp.max(tops[block], axis=0, keepdims=True) * SCALE_LOG2
 
     def weigh(step, at):
-        for lane in range(STEP):
-            pair = step * STEP + lane
+        for lane in range(WIDE):
+            pair = step * WIDE + lane
             i, j = at
             at = advance(at)
             shift = jnp.where(pair < pairs, shifts[i], FAR)

time: 56.2 us -> 55.9 us (level); the launches traced: 55.2 us -> 55.5 us
  transfers between devices with their start and end apart: 2 -> 2, of which waited for: 2 -> 2; matrix products, arithmetic and copies ran while one was open for 0% -> 0% of each run, Pallas kernels for 8% -> 9%
where the time goes in v9:
time: 55.9 us; the launch traced here: 55.5 us
  blocking collectives  31.9 us (57%)
  starting transfers between devices  9.96 us (18%)
  Pallas kernels  7.86 us (14%)
  waiting for transfers between devices  5.61 us (10%)
    all_to_all x2, blocking collectives, regrouped(): return lax.all_to_all(parts, ('core', 'grp'), 0, 0, tiled=True)  31.9 us
    ppermute x2, starting transfers between devices, exchanged(): return (part, lax.ppermute(part, ('sup', 'core'), pairs))  9.96 us
    ppermute x2, waiting for transfers between devices, exchanged(): return (part, lax.ppermute(part, ('sup', 'core'), pairs))  5.61 us
    pallas_call x1, Pallas kernels, own_part(): pl.pallas_call(own_kernel, out_shape=(jax.ShapeDtypeStruct((PER, WIDTH, B...  2.89 us
    pallas_call x1, Pallas kernels, halo_part(): pl.pallas_call(functools.partial(halo_kernel, turn), out_shape=jax.ShapeD...  1.96 us
    pallas_call x1, Pallas kernels, split_heads(): pl.pallas_call(functools.partial(split_kernel, counts), out_shape=[jax.Sh...  1.42 us
  transfers between devices with their start and end apart: 2, of which 2 were waited for; matrix products, arithmetic and copies ran while one was open for 0% of the time, Pallas kernels for 9%

profile of v9, /device:TPU:6, one launch (start us, length us, event | category | flops | bytes accessed | tf_op | source)
XLA Modules:
  0.0 55.5 jit_solution(10304870988530253745)
XLA Ops:
  0.0 20.5 %conditional.2 = (bf16[8,320,128]{2,1,0:T(8,128)(2,1)S(1)}, bf16[8,160,128]{2,1,0:T(8,128)(2,1)S(1)}) conditional(s32[]{:T(128)} %convert_element_type.4, (bf16[128,1280]{1,0:T(8,128)(2,1)}, bf16[128,1280]{1,0:T(8,128)(2,1)}, bf16[128,1280]{1,0:T(8,128)(2,1)}) %tuple.23, (bf16[128,1280]{1,0:T(8,128)(2,1)}, bf16[128,1280]{1,0:T(8,128)(2,1)}, ...), branch_computations={%region_0.0_spmd, %region_1.0_spmd} | conditional | flops 1500000000 | bytes 4932176 | solution.py:467
  0.0 1.4 %split_heads.2 = bf16[8,480,128]{2,1,0:T(8,128)(2,1)S(1)} custom-call(bf16[128,1280]{1,0:T(8,128)(2,1)} %get-tuple-element.24.refs_0_, bf16[128,1280]{1,0:T(8,128)(2,1)} %get-tuple-element.25.refs_1_, bf16[128,1280]{1,0:T(8,128)(2,1)} %get-tuple-element.26.refs_2_), custom_call_target="tpu_custom_call" | custom-call | flops 1500000000 | bytes 1000000 | tf_op jit(solution)/shard_map/cond/branch_0_fun/split_heads/pallas_call | solution.py:63
  1.4 19.0 %all_to_all.17 = bf16[8,480,128]{2,1,0:T(8,128)(2,1)S(1)} all-to-all(bf16[8,480,128]{2,1,0:T(8,128)(2,1)S(1)} %split_heads.2), channel_id=1, replica_groups=mesh['sup'=64,'core'=2,'grp'=4] {'core','grp'}, dimensions={0} | all-to-all | bytes 1966080 | tf_op jit(solution)/shard_map/cond/branch_0_fun/all_to_all | solution.py:452
  20.5 0.1 picked.2
  20.5 0.0 copy-start
  20.6 3.8 %collective-permute-start = (bf16[7,320,128]{2,1,0:T(8,128)(2,1)S(1)}, bf16[7,320,128]{2,1,0:T(8,128)(2,1)S(1)}, u32[]{:S(2)}, u32[]{:S(2)}) collective-permute-start(bf16[7,320,128]{2,1,0:T(8,128)(2,1)S(1)} %picked.2), channel_id=1, source_target_pairs={{0,8},{8,16},{16,24},{24,32},{32,40},{40,48},{48,56},{56,64},{64,7... | collective-permute-start | bytes 1720328 | tf_op jit(solution)/shard_map/ppermute | solution.py:448
  24.4 0.1 picked.3
  24.5 6.1 %collective-permute-start.1 = (bf16[7,320,128]{2,1,0:T(8,128)(2,1)S(1)}, bf16[7,320,128]{2,1,0:T(8,128)(2,1)S(1)}, u32[]{:S(2)}, u32[]{:S(2)}) collective-permute-start(bf16[7,320,128]{2,1,0:T(8,128)(2,1)S(1)} %picked.3), channel_id=1, source_target_pairs={{8,0},{16,8},{24,16},{32,24},{40,32},{48,40},{56,48},{64,56},{72,6... | collective-permute-start | bytes 1720328 | tf_op jit(solution)/shard_map/ppermute | solution.py:448
  30.6 0.0 copy-done
  30.6 2.9 %conditional.3 = (bf16[8,160,128]{2,1,0:T(8,128)(2,1)S(1)}, bf16[8,160,128]{2,1,0:T(8,128)(2,1)S(1)}, f32[8,160,128]{2,1,0:T(8,128)S(1)}, f32[8,1,256]{2,1,0:T(1,128)S(1)}, f32[8,1,256]{2,1,0:T(1,128)S(1)}) conditional(s32[]{:T(128)} %convert_element_type.4, (s32[512]{0:T(512)S(1)}, bf16[8,320,128]{2,1,0:T(8,128)(2,1)S(1)}, ...), branch_computations={%region_2.0_spmd, %region_3.0_spmd} | conditional | flops 99999997952 | bytes 2310198 | solution.py:480
  30.6 2.9 %own_part.1 = (bf16[8,160,128]{2,1,0:T(8,128)(2,1)S(1)}, f32[8,160,128]{2,1,0:T(8,128)S(1)}, f32[8,1,256]{2,1,0:T(1,128)S(1)}, f32[8,1,256]{2,1,0:T(1,128)S(1)}) custom-call(s32[512]{0:T(512)S(1)} %get-tuple-element.33.image_ref, bf16[8,320,128]{2,1,0:T(8,128)(2,1)S(1)} %get-tuple-element.34.kv_ref, bf16[8,160,128]{2,1,0:T(8,128)(2,1)S(1)} %get-tuple-element.61.q_ref), custom_call_target="tpu_custom_call" | custom-call | flops 99999997952 | bytes 1000000 | tf_op jit(solution)/shard_map/cond/branch_0_fun/own_part/pallas_call | solution.py:175
  33.5 3.9 %collective-permute-done.kv_ref.near_ref = bf16[7,320,128]{2,1,0:T(8,128)(2,1)S(1)} collective-permute-done((bf16[7,320,128]{2,1,0:T(8,128)(2,1)S(1)}, bf16[7,320,128]{2,1,0:T(8,128)(2,1)S(1)}, u32[]{:S(2)}, u32[]{:S(2)}) %collective-permute-start) | collective-permute-done | bytes 573472 | tf_op jit(solution)/shard_map/ppermute | solution.py:448
  37.4 2.0 %halo_part.1.start_ref = bf16[8,160,128]{2,1,0:T(8,128)(2,1)S(1)} custom-call(s32[512]{0:T(512)S(1)} %copy-done, bf16[7,320,128]{2,1,0:T(8,128)(2,1)S(1)} %collective-permute-done.kv_ref.near_ref, bf16[8,160,128]{2,1,0:T(8,128)(2,1)S(1)} %get-tuple-element.52.q_ref, bf16[8,160,128]{2,1,0:T(8,128)(2,1)S(1)} %get-tuple-element.53.start_ref, ...), custom_call_target="tpu_custom_call" | custom-call | flops 1000000000 | bytes 1000000 | tf_op jit(solution)/shard_map/halo_part/pallas_call | solution.py:283
  39.4 1.7 %collective-permute-done.1.far_ref = bf16[7,320,128]{2,1,0:T(8,128)(2,1)S(1)} collective-permute-done((bf16[7,320,128]{2,1,0:T(8,128)(2,1)S(1)}, bf16[7,320,128]{2,1,0:T(8,128)(2,1)S(1)}, u32[]{:S(2)}, u32[]{:S(2)}) %collective-permute-start.1) | collective-permute-done | bytes 573472 | tf_op jit(solution)/shard_map/ppermute | solution.py:448
  41.1 0.6 %last_part.1 = bf16[8,160,128]{2,1,0:T(8,128)(2,1)S(1)} custom-call(s32[512]{0:T(512)S(1)} %copy-done, bf16[8,320,128]{2,1,0:T(8,128)(2,1)S(1)} %get-tuple-element.49.kv_ref, bf16[7,320,128]{2,1,0:T(8,128)(2,1)S(1)} %collective-permute-done.kv_ref.near_ref, bf16[7,320,128]{2,1,0:T(8,128)(2,1)S(1)} %collective-permute-done.1.far_ref, ...), custom_call_target="tpu_custom_call" | custom-call | flops 1000000000 | bytes 1000000 | tf_op jit(solution)/shard_map/last_part/pallas_call | solution.py:399
  41.7 12.9 %all_to_all.20.in_ref = bf16[8,160,128]{2,1,0:T(8,128)(2,1)S(1)} all-to-all(bf16[8,160,128]{2,1,0:T(8,128)(2,1)S(1)} %last_part.1), channel_id=1, replica_groups=mesh['sup'=64,'core'=2,'grp'=4] {'core','grp'}, dimensions={0} | all-to-all | bytes 655360 | tf_op jit(solution)/shard_map/all_to_all | solution.py:452
  54.6 0.9 %join_heads.1 = bf16[128,1280]{1,0:T(8,128)(2,1)} custom-call(bf16[8,160,128]{2,1,0:T(8,128)(2,1)S(1)} %all_to_all.20.in_ref), custom_call_target="tpu_custom_call" | custom-call | tf_op jit(solution)/shard_map/join_heads/pallas_call | solution.py:83
  (2 shorter events, 0.1 us)
Async XLA Ops:
  20.5 10.0 %copy-start = (s32[512]{0:T(512)S(1)}, s32[512]{0:T(512)}, u32[]{:S(2)}) copy-start(s32[512]{0:T(512)} %image_ref.3) | copy-start | bytes 6148
  20.6 16.8 %collective-permute-start = (bf16[7,320,128]{2,1,0:T(8,128)(2,1)S(1)}, bf16[7,320,128]{2,1,0:T(8,128)(2,1)S(1)}, u32[]{:S(2)}, u32[]{:S(2)}) collective-permute-start(bf16[7,320,128]{2,1,0:T(8,128)(2,1)S(1)} %picked.2), channel_id=1, source_target_pairs={{0,8},{8,16},{16,24},{24,32},{32,40},{40,48},{48,56},{56,64},{64,7... | collective-permute-start | bytes 1720328 | tf_op jit(solution)/shard_map/ppermute | solution.py:448
  24.5 16.6 %collective-permute-start.1 = (bf16[7,320,128]{2,1,0:T(8,128)(2,1)S(1)}, bf16[7,320,128]{2,1,0:T(8,128)(2,1)S(1)}, u32[]{:S(2)}, u32[]{:S(2)}) collective-permute-start(bf16[7,320,128]{2,1,0:T(8,128)(2,1)S(1)} %picked.3), channel_id=1, source_target_pairs={{8,0},{16,8},{24,16},{32,24},{40,32},{48,40},{56,48},{64,56},{72,6... | collective-permute-start | bytes 1720328 | tf_op jit(solution)/shard_map/ppermute | solution.py:448
